TPU v7x, 256 devices: a whole 4x4x8 slice. The times are simulated.
256 devices in a mesh: tm: 8 (over z_lo, core), height: 8 (over z_hi, y), head: 4 (over x).
Axes of the slice: x: 4, y: 4, z: 8 (z_hi: 2, z_lo: 4; z = z_hi * 4 + z_lo), core: 2. Of those that a mesh axis runs over, the one named last changes fastest.
Arguments:
- latents: bfloat16 [16, 64, 16, 1152], P('tm', 'height', None, 'head'), may hold values from -45 to 45
- modulation: float32 [9, 1152], replicated, may hold values from -3 to 3
- spatial_qkv: bfloat16 [3, 1152, 1152], P(None, None, 'head'), may hold values from -2.563262 to 2.563262
- spatial_out: bfloat16 [1152, 1152], P('head'), may hold values from -1.5 to 1.5
- temporal_qkv: bfloat16 [3, 1152, 1152], P(None, None, 'head'), may hold values from -2.563262 to 2.563262
- temporal_out: bfloat16 [1152, 1152], P('head'), may hold values from -0.375 to 0.375
- mlp_up: bfloat16 [1152, 4608], P(None, 'head'), may hold values from -0.1875 to 0.1875
- mlp_down: bfloat16 [4608, 1152], P('head'), may hold values from -0.09375 to 0.09375
Outputs:
- result: bfloat16 [16, 64, 16, 1152], P('tm', 'height', None, 'head')
All inputs are finite; a program needn't handle non-finite values.
Results may differ from a plain program's by a relative error of at most 0.04.
Values may be sent and summed in bfloat16 or wider, within the bound.
A program may use at most 128 MiB of HBM per device.

v0:
```python
import jax
import jax.numpy as jnp
from jax import lax
from jax.sharding import PartitionSpec as P

D = 1152
HEAD_DIM = 72
TILE = 8


EPSILON = 1e-06


def extended(cells, sides, width):
    for axis, dim in sides:
        count = lax.axis_size(axis)
        ends = count - 1
        head = lax.slice_in_dim(cells, 0, width, axis=dim)
        tail = lax.slice_in_dim(cells, cells.shape[dim] - width, cells.shape[dim], axis=dim)
        cells = jnp.concatenate(
            [
                lax.ppermute(tail, axis, [(i, (i + 1) % count) for i in range(ends)]),
                cells,
                lax.ppermute(head, axis, [((i + 1) % count, i) for i in range(ends)]),
            ],
            axis=dim,
        )
    return cells


def modulate(values, shift_row, scale_row):
    data = values.astype(jnp.float32)
    mean_value = jnp.mean(data, axis=-1, keepdims=True)
    centred = data - mean_value
    variance = jnp.mean(centred * centred, axis=-1, keepdims=True)
    return (centred * lax.rsqrt(variance + EPSILON) * (1.0 + scale_row) + shift_row).astype(
        jnp.bfloat16
    )


def softmax_rows(scores):
    top_score = jnp.max(scores, axis=-1, keepdims=True)
    expo = jnp.exp(scores - top_score)
    return expo / jnp.sum(expo, axis=-1, keepdims=True)


def tile_form(tensor, tile_rows, tile_cols):
    frames_here = tensor.shape[0]
    width = tensor.shape[-1]
    shaped = tensor.reshape(frames_here, tile_rows, TILE, tile_cols, TILE, width)
    return shaped.transpose(0, 1, 3, 2, 4, 5).reshape(
        frames_here, tile_rows, tile_cols, TILE * TILE, width
    )


def grid_form(tensor, tile_rows, tile_cols):
    frames_here = tensor.shape[0]
    width = tensor.shape[-1]
    shaped = tensor.reshape(frames_here, tile_rows, tile_cols, TILE, TILE, width)
    return shaped.transpose(0, 1, 3, 2, 4, 5).reshape(
        frames_here, tile_rows * TILE, tile_cols * TILE, width
    )


def neighbourhood(padded, tile_rows, tile_cols):
    grid_tiles = tile_form(padded, tile_rows + 2, tile_cols + 2)
    pieces = [
        grid_tiles[:, row_step : row_step + tile_rows, col_step : col_step + tile_cols]
        for row_step in range(3)
        for col_step in range(3)
    ]
    stacked = jnp.stack(pieces, axis=3)
    return stacked.reshape(padded.shape[0], tile_rows, tile_cols, 9 * TILE * TILE, padded.shape[-1])


def tile_mask(tile_rows, tile_cols, row_base, total_rows):
    order = jnp.arange(9)
    row_step = order // 3 - 1
    col_step = order % 3 - 1
    rows_at = row_base + jnp.arange(tile_rows)[:, None, None] + row_step[None, None, :]
    cols_at = jnp.arange(tile_cols)[None, :, None] + col_step[None, None, :]
    valid = (rows_at >= 0) & (rows_at < total_rows) & (cols_at >= 0) & (cols_at < tile_cols)
    return jnp.repeat(valid, TILE * TILE, axis=2)


def spatial_attend(queries, key_field, value_field, row_base, total_rows):
    frames_here, rows_here, cols_here, width = queries.shape
    heads_here = width // HEAD_DIM
    tile_rows = rows_here // TILE
    tile_cols = cols_here // TILE
    query_tiles = tile_form(queries, tile_rows, tile_cols).reshape(
        frames_here, tile_rows, tile_cols, TILE * TILE, heads_here, HEAD_DIM
    )
    padding = ((0, 0), (0, 0), (TILE, TILE), (0, 0))
    key_tiles = neighbourhood(jnp.pad(key_field, padding), tile_rows, tile_cols).reshape(
        frames_here, tile_rows, tile_cols, 9 * TILE * TILE, heads_here, HEAD_DIM
    )
    value_tiles = neighbourhood(jnp.pad(value_field, padding), tile_rows, tile_cols).reshape(
        frames_here, tile_rows, tile_cols, 9 * TILE * TILE, heads_here, HEAD_DIM
    )
    scores = jnp.einsum(
        "fabqhd,fabkhd->fabhqk", query_tiles, key_tiles, preferred_element_type=jnp.float32
    ) * HEAD_DIM ** (-0.5)
    valid = tile_mask(tile_rows, tile_cols, row_base, total_rows)[None, :, :, None, None, :]
    scores = jnp.where(valid, scores, -1e30)
    weights = softmax_rows(scores).astype(jnp.bfloat16)
    mixed = jnp.einsum(
        "fabhqk,fabkhd->fabqhd", weights, value_tiles, preferred_element_type=jnp.float32
    ).astype(jnp.bfloat16)
    mixed = mixed.reshape(frames_here, tile_rows, tile_cols, TILE * TILE, width)
    return grid_form(mixed, tile_rows, tile_cols)


def temporal_attend(queries, key_field, value_field):
    frames_all, tokens_here, width = queries.shape
    heads_here = width // HEAD_DIM
    shape_heads = (frames_all, tokens_here, heads_here, HEAD_DIM)
    scores = jnp.einsum(
        "qthd,kthd->thqk",
        queries.reshape(shape_heads),
        key_field.reshape(shape_heads),
        preferred_element_type=jnp.float32,
    ) * HEAD_DIM ** (-0.5)
    weights = softmax_rows(scores).astype(jnp.bfloat16)
    mixed = jnp.einsum(
        "thqk,kthd->qthd",
        weights,
        value_field.reshape(shape_heads),
        preferred_element_type=jnp.float32,
    )
    return mixed.astype(jnp.bfloat16).reshape(frames_all, tokens_here, width)


def merge_branch(partial_value, base_part, gate_row, offset, part_width):
    shares = lax.psum_scatter(
        partial_value.astype(jnp.bfloat16), "head", scatter_dimension=3, tiled=True
    ).astype(jnp.float32)
    gate_part = lax.dynamic_slice_in_dim(gate_row, offset, part_width)
    own_part = (base_part.astype(jnp.float32) + gate_part * shares).astype(jnp.bfloat16)
    full_rows = lax.all_gather(own_part, "head", axis=3, tiled=True)
    return (own_part, full_rows)


def body(
    latents, modulation, spatial_qkv, spatial_out, temporal_qkv, temporal_out, mlp_up, mlp_down
):
    frames_dev, rows_dev, cols_dev, part_width = latents.shape
    offset = lax.axis_index("head") * part_width
    tile_rows = rows_dev // TILE
    row_base = lax.axis_index("height") * tile_rows
    total_rows = tile_rows * lax.axis_size("height")
    full_rows = lax.all_gather(latents, "head", axis=3, tiled=True)
    normed = modulate(full_rows, modulation[0], modulation[1])
    projected = jnp.einsum(
        "frcd,sde->sfrce", normed, spatial_qkv, preferred_element_type=jnp.float32
    ).astype(jnp.bfloat16)
    queries = projected[0]
    key_value = extended(projected[1:], (("height", 2),), TILE)
    attended = spatial_attend(queries, key_value[0], key_value[1], row_base, total_rows)
    partial_value = jnp.dot(
        attended.reshape(-1, part_width), spatial_out, preferred_element_type=jnp.float32
    ).reshape(frames_dev, rows_dev, cols_dev, -1)
    first_part, first_full = merge_branch(partial_value, latents, modulation[2], offset, part_width)
    normed = modulate(first_full, modulation[3], modulation[4])
    projected = jnp.einsum(
        "frcd,sde->sfrce", normed, temporal_qkv, preferred_element_type=jnp.float32
    ).astype(jnp.bfloat16)
    projected = projected.reshape(3, frames_dev, rows_dev * cols_dev, part_width)
    triple = (projected[0], projected[1], projected[2])
    arrived = (
        lax.all_to_all(triple[0], "tm", split_axis=1, concat_axis=0, tiled=True),
        lax.all_to_all(triple[1], "tm", split_axis=1, concat_axis=0, tiled=True),
        lax.all_to_all(triple[2], "tm", split_axis=1, concat_axis=0, tiled=True),
    )
    mixed = temporal_attend(arrived[0], arrived[1], arrived[2])
    returned = lax.all_to_all(mixed, "tm", split_axis=0, concat_axis=1, tiled=True)
    partial_value = jnp.dot(
        returned.reshape(-1, part_width), temporal_out, preferred_element_type=jnp.float32
    ).reshape(frames_dev, rows_dev, cols_dev, -1)
    second_part, second_full = merge_branch(
        partial_value, first_part, modulation[5], offset, part_width
    )
    normed = modulate(second_full, modulation[6], modulation[7])
    hidden = jax.nn.gelu(
        jnp.dot(normed.reshape(-1, D), mlp_up, preferred_element_type=jnp.float32), approximate=True
    ).astype(jnp.bfloat16)
    partial_value = jnp.dot(hidden, mlp_down, preferred_element_type=jnp.float32).reshape(
        frames_dev, rows_dev, cols_dev, -1
    )
    shares = lax.psum_scatter(
        partial_value.astype(jnp.bfloat16), "head", scatter_dimension=3, tiled=True
    ).astype(jnp.float32)
    gate_part = lax.dynamic_slice_in_dim(modulation[8], offset, part_width)
    return (second_part.astype(jnp.float32) + gate_part * shares).astype(jnp.bfloat16)


def solution(mesh):
    return jax.shard_map(
        body,
        mesh=mesh,
        in_specs=(
            P("tm", "height", None, "head"),
            P(),
            P(None, None, "head"),
            P("head", None),
            P(None, None, "head"),
            P("head", None),
            P(None, "head"),
            P("head", None),
        ),
        out_specs=P("tm", "height", None, "head"),
        check_vma=False,
    )
```

profile of v0, /device:TPU:1, one launch (start us, length us, event | category | flops | bytes accessed | tf_op | source)
XLA Modules:
  0.0 454.0 jit_solution(15308632702801721894)
XLA Ops:
  9.7 52.3 %all_gather.9 = bf16[2,8,16,1152]{2,1,0,3:T(8,128)(2,1)} all-gather(bf16[2,8,16,288]{2,1,0,3:T(8,128)(2,1)} %copy.177), channel_id=1, replica_groups=mesh['tm'=8,'height'=8,'head'=4] {'head'}, dimensions={3}, use_global_device_ids=true | all-gather | bytes 737280 | tf_op jit(solution)/shard_map/all_gather | solution.py:152
  62.0 4.8 %copy.178 = bf16[2,8,16,1152]{3,2,1,0:T(8,128)(2,1)S(1)} copy(bf16[2,8,16,1152]{2,1,0,3:T(8,128)(2,1)} %all_gather.9) | data formatting | bytes 1179648 | tf_op jit(solution)/shard_map/all_gather | solution.py:152
  72.7 4.8 %collective-permute-start = (bf16[2,2,8,16,288]{4,3,0,2,1:T(8,128)(2,1)S(1)}, bf16[2,2,8,16,288]{4,3,0,2,1:T(8,128)(2,1)}, u32[]{:S(2)}, u32[]{:S(2)}) collective-permute-start(bf16[2,2,8,16,288]{4,3,0,2,1:T(8,128)(2,1)S(1)} %slice.139), channel_id=1, source_target_pairs={{0,4},{4,8},{8,12},{12,16},{16,20},{20,24},{24,28},{1,5},{5,9},{9,... | collective-permute-start | bytes 884744 | tf_op jit(solution)/shard_map/ppermute | solution.py:22
  91.7 7.2 %copy.229 = bf16[2,1,2,9,64,288]{4,3,5,2,0,1:T(8,128)(2,1)} copy(bf16[2,1,2,9,64,288]{5,4,2,0,3,1:T(8,128)(2,1)} %fusion.88) | data formatting | bytes 2654208 | tf_op jit(solution)/shard_map/reshape.13
  98.9 6.2 %reshape.243 = bf16[2,2,576,4,72]{2,4,3,1,0:T(8,128)(2,1)} reshape(bf16[2,1,2,9,64,288]{4,3,5,2,0,1:T(8,128)(2,1)} %copy.229) | data formatting | bytes 2654208 | tf_op jit(solution)/shard_map/reshape.13
  111.7 7.2 %copy.230 = bf16[2,1,2,9,64,288]{4,3,5,2,0,1:T(8,128)(2,1)} copy(bf16[2,1,2,9,64,288]{5,4,2,0,3,1:T(8,128)(2,1)} %fusion.79) | data formatting | bytes 2654208 | tf_op jit(solution)/shard_map/reshape.9
  118.9 6.3 %reshape.244 = bf16[2,2,576,4,72]{2,4,3,1,0:T(8,128)(2,1)} reshape(bf16[2,1,2,9,64,288]{4,3,5,2,0,1:T(8,128)(2,1)} %copy.230) | data formatting | bytes 2654208 | tf_op jit(solution)/shard_map/reshape.9
  138.5 6.9 %reshape.245 = bf16[1152,256]{1,0:T(8,128)(2,1)} reshape(bf16[1152,2,8,16]{3,2,1,0:T(8,128)(2,1)} %bitcast.228) | data formatting | bytes 1179648
  145.5 39.6 %reduce-scatter.10.cloned.1.call-done = bf16[288,256]{1,0:T(8,128)(2,1)} async-done(((bf16[1152,256]{1,0:T(8,128)(2,1)}), bf16[288,256]{1,0:T(8,128)(2,1)}) %reduce-scatter.10.cloned.1.call-update) | async-done | bytes 147472
  192.1 48.3 %all_gather.10 = bf16[2,8,16,1152]{2,1,0,3:T(8,128)(2,1)} all-gather(bf16[2,8,16,288]{2,1,0,3:T(8,128)(2,1)} %copy.203), channel_id=1, replica_groups=mesh['tm'=8,'height'=8,'head'=4] {'head'}, dimensions={3}, use_global_device_ids=true | all-gather | bytes 737280 | tf_op jit(solution)/shard_map/all_gather | solution.py:140
  240.4 4.8 %copy.204 = bf16[2,8,16,1152]{3,2,1,0:T(8,128)(2,1)S(1)} copy(bf16[2,8,16,1152]{2,1,0,3:T(8,128)(2,1)} %all_gather.10) | data formatting | bytes 1179648 | tf_op jit(solution)/shard_map/all_gather | solution.py:140
  249.3 7.5 %all-to-all-start.2 = ((bf16[2,128,288]{2,0,1:T(2,128)(2,1)}), bf16[2,128,288]{2,0,1:T(2,128)(2,1)S(1)}, u32[]{:S(2)}, u32[]{:S(2)}) async-start(bf16[2,128,288]{2,0,1:T(2,128)(2,1)} %copy.211), calls=%async_computation.2 | async-start | bytes 393216 | tf_op jit(solution)/shard_map/all_to_all | solution.py:172
  257.7 5.6 %all-to-all-done.2 = bf16[2,128,288]{2,0,1:T(2,128)(2,1)S(1)} async-done(((bf16[2,128,288]{2,0,1:T(2,128)(2,1)}), bf16[2,128,288]{2,0,1:T(2,128)(2,1)S(1)}, u32[]{:S(2)}, u32[]{:S(2)}) %all-to-all-start.2) | async-done | bytes 147488 | tf_op jit(solution)/shard_map/all_to_all | solution.py:172
  263.3 5.8 %all-to-all-start.1 = ((bf16[2,128,288]{2,0,1:T(2,128)(2,1)}), bf16[2,128,288]{2,0,1:T(2,128)(2,1)}, u32[]{:S(2)}, u32[]{:S(2)}) async-start(bf16[2,128,288]{2,0,1:T(2,128)(2,1)} %copy.208), calls=%async_computation.1 | async-start | bytes 393216 | tf_op jit(solution)/shard_map/all_to_all | solution.py:171
  270.2 5.5 %all-to-all-done.1 = bf16[2,128,288]{2,0,1:T(2,128)(2,1)} async-done(((bf16[2,128,288]{2,0,1:T(2,128)(2,1)}), bf16[2,128,288]{2,0,1:T(2,128)(2,1)}, u32[]{:S(2)}, u32[]{:S(2)}) %all-to-all-start.1) | async-done | bytes 147488 | tf_op jit(solution)/shard_map/all_to_all | solution.py:171
  275.6 5.8 %all-to-all-start = ((bf16[2,128,288]{2,0,1:T(2,128)(2,1)}), bf16[2,128,288]{2,0,1:T(2,128)(2,1)}, u32[]{:S(2)}, u32[]{:S(2)}) async-start(bf16[2,128,288]{2,0,1:T(2,128)(2,1)} %copy.205), calls=%async_computation | async-start | bytes 393216 | tf_op jit(solution)/shard_map/all_to_all | solution.py:173
  292.8 10.7 %all_to_all.60 = bf16[16,16,288]{2,1,0:T(8,128)(2,1)S(1)} all-to-all(bf16[16,16,288]{2,1,0:T(8,128)(2,1)S(1)} %reshape.235), channel_id=1, replica_groups=mesh['tm'=8,'height'=8,'head'=4] {'tm'}, dimensions={0} | all-to-all | bytes 294912 | tf_op jit(solution)/shard_map/all_to_all | solution.py:176
  305.1 4.6 %copy.233 = bf16[2,8,16,1152]{2,1,0,3:T(8,128)(2,1)} copy(bf16[2,8,16,1152]{3,2,1,0:T(8,128)(2,1)S(1)} %convolution_convert_fusion.1) | data formatting | bytes 1179648
  309.7 6.9 %reshape.247 = bf16[1152,256]{1,0:T(8,128)(2,1)} reshape(bf16[1152,2,8,16]{3,2,1,0:T(8,128)(2,1)} %bitcast.229) | data formatting | bytes 1179648
  316.7 22.9 %reduce-scatter.12.cloned.1.call-done = bf16[288,256]{1,0:T(8,128)(2,1)} async-done(((bf16[1152,256]{1,0:T(8,128)(2,1)}), bf16[288,256]{1,0:T(8,128)(2,1)}) %reduce-scatter.12.cloned.1.call-update) | async-done | bytes 147472
  346.6 48.2 %all_gather.11 = bf16[2,8,16,1152]{2,1,0,3:T(8,128)(2,1)} all-gather(bf16[2,8,16,288]{2,1,0,3:T(8,128)(2,1)} %copy.220), channel_id=1, replica_groups=mesh['tm'=8,'height'=8,'head'=4] {'head'}, dimensions={3}, use_global_device_ids=true | all-gather | bytes 737280 | tf_op jit(solution)/shard_map/all_gather | solution.py:140
  394.8 4.8 %copy.221 = bf16[2,8,16,1152]{3,2,1,0:T(8,128)(2,1)S(1)} copy(bf16[2,8,16,1152]{2,1,0,3:T(8,128)(2,1)} %all_gather.11) | data formatting | bytes 1179648 | tf_op jit(solution)/shard_map/all_gather | solution.py:140
  409.6 6.9 %reshape.249 = bf16[1152,256]{1,0:T(8,128)(2,1)} reshape(bf16[1152,2,8,16]{3,2,1,0:T(8,128)(2,1)} %bitcast.230) | data formatting | bytes 1179648
  416.6 25.3 %reduce-scatter.14.cloned.1.call-done = bf16[288,256]{1,0:T(8,128)(2,1)} async-done(((bf16[1152,256]{1,0:T(8,128)(2,1)}), bf16[288,256]{1,0:T(8,128)(2,1)}) %reduce-scatter.14.cloned.1.call-update) | async-done | bytes 147472
  (115 shorter events, 91.7 us)
Async XLA Ops:
  6.5 394.7 %copy-start = (bf16[1152,1152]{1,0:T(8,128)(2,1)S(1)}, bf16[1152,1152]{1,0:T(8,128)(2,1)}, u32[]{:S(2)}) copy-start(bf16[1152,1152]{1,0:T(8,128)(2,1)} %param.15) | copy-start | bytes 7962628
  6.5 178.6 %reduce-scatter.10.cloned.1.call-start = ((), (), s32[]{:S(2)}) async-start(), calls=%async_computation.7 | async-start | bytes 737280
  61.9 4.9 %copy-start.5 = (f32[9,1152]{1,0:T(8,128)S(1)}, f32[9,1152]{1,0:T(8,128)}, u32[]{:S(2)}) copy-start(f32[9,1152]{1,0:T(8,128)} %param.9) | copy-start | bytes 124420
  70.6 0.8 copy-start.4
  71.4 11.4 %collective-permute-start.1 = (bf16[2,2,8,16,288]{4,3,0,2,1:T(8,128)(2,1)S(1)}, bf16[2,2,8,16,288]{4,3,0,2,1:T(8,128)(2,1)}, u32[]{:S(2)}, u32[]{:S(2)}) collective-permute-start(bf16[2,2,8,16,288]{4,3,0,2,1:T(8,128)(2,1)S(1)} %slice.139), channel_id=1, source_target_pairs={{4,0},{8,4},{12,8},{16,12},{20,16},{24,20},{28,24},{5,1},{9,5},{13... | collective-permute-start | bytes 884744 | tf_op jit(solution)/shard_map/ppermute | solution.py:24
  72.7 10.9 %collective-permute-start = (bf16[2,2,8,16,288]{4,3,0,2,1:T(8,128)(2,1)S(1)}, bf16[2,2,8,16,288]{4,3,0,2,1:T(8,128)(2,1)}, u32[]{:S(2)}, u32[]{:S(2)}) collective-permute-start(bf16[2,2,8,16,288]{4,3,0,2,1:T(8,128)(2,1)S(1)} %slice.139), channel_id=1, source_target_pairs={{0,4},{4,8},{8,12},{12,16},{16,20},{20,24},{24,28},{1,5},{5,9},{9,... | collective-permute-start | bytes 884744 | tf_op jit(solution)/shard_map/ppermute | solution.py:22
  118.9 6.3 %copy-start.7 = (pred[2,576]{1,0:T(4,128)(4,1)S(1)}, pred[2,576]{1,0:T(4,128)(4,1)}, u32[]{:S(2)}) copy-start(pred[2,576]{1,0:T(4,128)(4,1)} %broadcast_in_dim.17) | copy-start | bytes 3460
  145.4 44.5 %copy-start.3 = (bf16[2,8,16,288]{3,2,1,0:T(8,128)(2,1)S(1)}, bf16[2,8,16,288]{3,2,1,0:T(8,128)(2,1)}, u32[]{:S(2)}) copy-start(bf16[2,8,16,288]{3,2,1,0:T(8,128)(2,1)} %param.8) | copy-start | bytes 442372
  240.4 5.3 %copy-start.6 = (f32[1152]{0:T(1024)S(1)}, f32[1152]{0:T(1024)}, u32[]{:S(2)}) copy-start(f32[1152]{0:T(1024)} %get-tuple-element.23) | copy-start | bytes 13828
  249.3 14.0 %all-to-all-start.2 = ((bf16[2,128,288]{2,0,1:T(2,128)(2,1)}), bf16[2,128,288]{2,0,1:T(2,128)(2,1)S(1)}, u32[]{:S(2)}, u32[]{:S(2)}) async-start(bf16[2,128,288]{2,0,1:T(2,128)(2,1)} %copy.211), calls=%async_computation.2 | async-start | bytes 393216 | tf_op jit(solution)/shard_map/all_to_all | solution.py:172
  263.3 12.3 %all-to-all-start.1 = ((bf16[2,128,288]{2,0,1:T(2,128)(2,1)}), bf16[2,128,288]{2,0,1:T(2,128)(2,1)}, u32[]{:S(2)}, u32[]{:S(2)}) async-start(bf16[2,128,288]{2,0,1:T(2,128)(2,1)} %copy.208), calls=%async_computation.1 | async-start | bytes 393216 | tf_op jit(solution)/shard_map/all_to_all | solution.py:171
  275.6 12.4 %all-to-all-start = ((bf16[2,128,288]{2,0,1:T(2,128)(2,1)}), bf16[2,128,288]{2,0,1:T(2,128)(2,1)}, u32[]{:S(2)}, u32[]{:S(2)}) async-start(bf16[2,128,288]{2,0,1:T(2,128)(2,1)} %copy.205), calls=%async_computation | async-start | bytes 393216 | tf_op jit(solution)/shard_map/all_to_all | solution.py:173
  281.4 58.1 %reduce-scatter.12.cloned.1.call-start = ((), (), s32[]{:S(2)}) async-start(), calls=%async_computation.8 | async-start | bytes 737280
  316.6 125.3 %reduce-scatter.14.cloned.1.call-start = ((), (), s32[]{:S(2)}) async-start(), calls=%async_computation.9 | async-start | bytes 737280
  344.5 2.1 copy-start.1
  416.5 30.2 %copy-start.2 = (bf16[2,8,16,288]{3,2,1,0:T(8,128)(2,1)S(1)}, bf16[2,8,16,288]{3,2,1,0:T(8,128)(2,1)}, u32[]{:S(2)}) copy-start(bf16[2,8,16,288]{3,2,1,0:T(8,128)(2,1)} %copy-done.1) | copy-start | bytes 442372
Sparse Core Ops, SparseCore 0:
  145.5 39.5 reduce-scatter.9
  316.7 22.7 reduce-scatter.11
  416.7 25.1 reduce-scatter.13
where the time goes:
time: 459 us; the launch traced here: 454 us
  blocking collectives  160 us (35%)
  local copies, waits for them, and re-layouts  122 us (27%)
  waiting for transfers between devices  105 us (23%)
  starting transfers between devices  25.2 us (5%)
  matrix products  23 us (5%)
  between operations  13.5 us (3%)
  other arithmetic  5.4 us (1%)
    all_gather x2, blocking collectives, merge_branch(): full_rows = lax.all_gather(own_part, 'head', axis=3, tiled=True)  96.5 us
    unnamed x6, waiting for transfers between devices  87.8 us
    unnamed x45, local copies, waits for them, and re-layouts  64.2 us
    all_gather x1, blocking collectives, body(): full_rows = lax.all_gather(latents, 'head', axis=3, tiled=True)  52.3 us
    another operation x5, local copies, waits for them, and re-layouts  27 us
    all_to_all x1, blocking collectives, body(): lax.all_to_all(mixed, 'tm', split_axis=0, concat_axis=1, tiled=True)  10.7 us
    all_gather x2, local copies, waits for them, and re-layouts, merge_branch(): full_rows = lax.all_gather(own_part, 'head', axis=3, tiled=True)  9.64 us
  transfers between devices with their start and end apart: 8, of which 8 were waited for; matrix products, arithmetic and copies ran while one was open for 2% of the time, Pallas kernels for 0%

commit v1 on v0

v1 whole, which is shorter than its diff:
```python
import functools

import jax
import jax.numpy as jnp
from jax import lax
from jax.experimental import pallas as pl
from jax.experimental.pallas import tpu as pltpu
from jax.sharding import PartitionSpec as P

D = 1152
HEAD_DIM = 72
PART = 288
COVER = 384
HEADS = 4
EPSILON = 1e-06
SCALE = HEAD_DIM ** (-0.5)
MESH = pl.DeviceIdType.MESH
F32 = jnp.float32
BF16 = jnp.bfloat16


def dot(a, b):
    return jnp.dot(a, b, preferred_element_type=F32)


def dot_t(a, b):
    return lax.dot_general(a, b, (((1,), (1,)), ((), ())), preferred_element_type=F32)


def modulate(v, shift, scale):
    mean = jnp.mean(v, axis=-1, keepdims=True)
    cen = v - mean
    var = jnp.mean(cen * cen, axis=-1, keepdims=True)
    return (cen * lax.rsqrt(var + EPSILON) * (1.0 + scale) + shift).astype(BF16)


def one_hot(rows, cols, source):
    r = lax.broadcasted_iota(jnp.int32, (rows, cols), 0)
    s = lax.broadcasted_iota(jnp.int32, (rows, cols), 1)
    return jnp.where(source(r) == s, 1.0, 0.0).astype(BF16)


def head_masks():
    lane = lax.broadcasted_iota(jnp.int32, (1, PART), 1)
    return [
        jnp.where((lane >= HEAD_DIM * h) & (lane < HEAD_DIM * (h + 1)), 1.0, 0.0).astype(F32)
        for h in range(HEADS)
    ]


def stack_heads(q, masks):
    q = q.astype(F32)
    return jnp.concatenate([(q * m).astype(BF16) for m in masks], axis=0)


def pick_heads(o, masks):
    n = o.shape[0] // HEADS
    total = o[0:n] * masks[0]
    for h in range(1, HEADS):
        total = total + o[h * n : (h + 1) * n] * masks[h]
    return total.astype(BF16)


def softmax(s):
    top = jnp.max(s, axis=-1, keepdims=True)
    e = jnp.exp(s - top)
    return (e / jnp.sum(e, axis=-1, keepdims=True)).astype(BF16)


def kernel(
    lat, mod, wqkv_h, wo_h, tqkv_h, to_h, up_h, dn_h, o_ref,
    w_s, w_so, w_t, w_to, w_up, w_dn,
    g, lfull, nrm, qb, kvo, inn, outr, ps, r4, lsel, fst, pk, a2, blk, att, pt, r7, blk2, hid, pm, r8, fin,
    wsem, s1, d1, sh, dh, s4, d4, s5, d5, s6, d6, s7, d7, s7b, d7b, s8, d8, s9, d9,
):
    tm = lax.axis_index("tm")
    he = lax.axis_index("height")
    x = lax.axis_index("head")
    zlo, c = tm // 2, tm % 2
    zhi, y = he // 4, he % 4
    d = (y + 4 - 2 * c) % 4
    w = d // 2
    t_me = ((d + 1) // 2) % 2
    m_me = 8 * t_me + 4 * w + zlo
    f_me = 4 * zlo + y
    at_home = y // 2 == c
    cross = zhi != c

    def dev(zlo, c, zhi, y, x):
        return (zlo * 2 + c, zhi * 4 + y, x)

    def xdev(k):
        return (tm, he, (x + k) % 4)

    def group_dev(m):
        tt, ww, zz = m // 8, (m // 4) % 2, m % 4
        return (zz * 2 + c, zhi * 4 + (2 * c + tt + ww * (2 * tt - 1) + 4) % 4, x)

    def remote(src, dst, ssem, rsem, device):
        return pltpu.make_async_remote_copy(
            src_ref=src, dst_ref=dst, send_sem=ssem, recv_sem=rsem, device_id=device, device_id_type=MESH
        )

    def arrived(dst, rsem):
        pltpu.make_async_copy(dst, dst, rsem).wait()

    loads = [
        pltpu.make_async_copy(wqkv_h, w_s, wsem.at[0]),
        pltpu.make_async_copy(wo_h, w_so, wsem.at[1]),
        pltpu.make_async_copy(tqkv_h, w_t, wsem.at[2]),
        pltpu.make_async_copy(to_h, w_to, wsem.at[3]),
        pltpu.make_async_copy(up_h, w_up, wsem.at[4]),
        pltpu.make_async_copy(dn_h, w_dn, wsem.at[5]),
    ]
    for load in loads:
        load.start()

    bar = pltpu.get_barrier_semaphore()

    def tell(device):
        pl.semaphore_signal(bar, inc=1, device_id=device, device_id_type=MESH)

    def first_peer(i, k):
        return dev(zlo, y // 2, zhi, 2 * c + i, (x + k) % 4)

    for k in range(1, 4):
        tell(xdev(k))
        for i in range(2):
            tell(first_peer(i, k))
    tell(dev(zlo, 1 - c, zhi, y, x))
    for k in range(1, 16):
        tell(group_dev((m_me + k) % 16))

    @pl.when(cross)
    def _():
        tell(dev(zlo, 1 - c, 1 - zhi, y, x))

    @pl.when(jnp.logical_not(at_home))
    def _():
        for i in range(2):
            tell(first_peer(i, 0))
        for z in range(4):
            tell(dev(z, 1 - c, zhi, y, x))
            tell(dev(z, 1 - c, zhi, (2 * (1 - c) + 3 * (y % 2) + 3) % 4, x))

    pl.semaphore_wait(
        bar, 9 + 1 + 15 + 4 + jnp.where(cross, 1, 0) + jnp.where(at_home, 0, 2)
    )

    slot = y % 2

    def first_copy(i, k):
        return remote(lat.at[i], g.at[x, slot], s1.at[i * 4 + k], d1.at[x * 2 + slot], first_peer(i, k))

    for k in (2, 1, 3):
        for i in range(2):
            first_copy(i, k).start()

    @pl.when(at_home)
    def _():
        pltpu.make_async_copy(lat.at[slot], g.at[x, slot], d1.at[x * 2 + slot]).start()
        first_copy(1 - slot, 0).start()

    @pl.when(jnp.logical_not(at_home))
    def _():
        first_copy(0, 0).start()
        first_copy(1, 0).start()

    masks = head_masks()
    order = one_hot(128, 128, lambda r: 16 * ((r % 32) // 4) + 4 * (r // 32) + r % 4)
    chosen = one_hot(32, 128, lambda r: 16 * (r // 4) + 4 * x + r % 4)

    @pl.when(jnp.logical_not(cross))
    def _():
        outr[...] = jnp.zeros_like(outr)

    for s in range(2):
        for xs in range(4):
            arrived(g.at[xs, s], d1.at[xs * 2 + s])
        whole = jnp.concatenate([g[xs, s].astype(F32) for xs in range(4)], axis=1)
        lfull[s * 128 : (s + 1) * 128] = whole.astype(BF16)
        nrm[s * 128 : (s + 1) * 128] = modulate(whole, mod[0:1], mod[1:2])

    loads[0].wait()
    kvo[0] = dot(nrm[...], w_s[1]).astype(BF16)
    kvo[1] = dot(nrm[...], w_s[2]).astype(BF16)
    row_a, row_b = 1 - c, c
    inner = remote(
        kvo.at[:, pl.ds(row_a * 128, 128)], inn, sh.at[0], dh.at[0], dev(zlo, 1 - c, zhi, y, x)
    )
    outer = remote(
        kvo.at[:, pl.ds(row_b * 128, 128)], outr, sh.at[1], dh.at[1], dev(zlo, 1 - c, 1 - zhi, y, x)
    )

    @pl.when(cross)
    def _():
        outer.start()

    inner.start()
    queries = dot(nrm[...], w_s[0]).astype(BF16)
    for s in range(2):
        qb[s] = dot(order, queries[s * 128 : (s + 1) * 128]).astype(BF16)
        lsel[s] = dot(chosen, lfull[s * 128 : (s + 1) * 128]).astype(BF16)
    loads[1].wait()

    def spatial(t, extra, bias):
        q4 = stack_heads(qb[t], masks)
        own = dot_t(q4, kvo[0]) * SCALE
        far = dot_t(q4, extra[0]) * SCALE + bias
        p = softmax(jnp.concatenate([own, far], axis=1))
        o = dot(p[:, :256], kvo[1]) + dot(p[:, 256:], extra[1])
        ps[t] = dot(pick_heads(o, masks), w_so[...]).astype(BF16)

    def spatial_send(n, t, k):
        return remote(
            ps.at[t, pl.ds(((x + k) % 4) * 32, 32)], r4.at[x, t], s4.at[n * 4 + k], d4.at[x * 2 + t], xdev(k)
        )

    arrived(inn, dh.at[0])
    spatial(row_a, inn, 0.0)
    for k in (2, 1, 3):
        spatial_send(0, row_a, k).start()

    @pl.when(cross)
    def _():
        arrived(outr, dh.at[1])

    spatial(row_b, outr, jnp.where(cross, 0.0, -1e30))
    for k in (2, 1, 3):
        spatial_send(1, row_b, k).start()

    for t in (row_a, row_b):
        total = ps[t, pl.ds(x * 32, 32)].astype(F32)
        for k in (1, 3, 2):
            xs = (x + k) % 4
            arrived(r4.at[xs, t], d4.at[xs * 2 + t])
            total = total + r4[xs, t].astype(F32)
        fst[t] = (lsel[t].astype(F32) + mod[2:3] * total).astype(BF16)

    rows = jnp.concatenate([fst[0], fst[1]], axis=0)
    packed = jnp.zeros((256, COVER), F32)
    for j in range(3):
        r = lax.broadcasted_iota(jnp.int32, (256, 64), 0)
        s = lax.broadcasted_iota(jnp.int32, (256, 64), 1)
        sel = jnp.where((r // 16 == s // 4) & ((r % 16) // 4 == j) & (r % 4 == s % 4), 1.0, 0.0).astype(BF16)
        packed = packed + dot(sel, rows[:, j * COVER : (j + 1) * COVER])
    pk[...] = packed.astype(BF16).reshape(16, 16, COVER)

    def spread(k):
        m = (m_me + k) % 16
        return remote(pk.at[m], a2.at[f_me], s5.at[k], d5.at[f_me], group_dev(m))

    for k in range(1, 16):
        spread(k).start()
    a2[f_me] = pk[m_me]
    for k in range(1, 16):
        f = (f_me + k) % 16
        arrived(a2.at[f], d5.at[f])
    flat = a2[...].reshape(256, COVER)
    for j in range(3):
        r = lax.broadcasted_iota(jnp.int32, (64, 256), 0)
        s = lax.broadcasted_iota(jnp.int32, (64, 256), 1)
        sel = jnp.where((s // 16 == r // 4) & ((s % 16) // 4 == j) & (r % 4 == s % 4), 1.0, 0.0).astype(BF16)
        blk[x, :, j * COVER : (j + 1) * COVER] = dot(sel, flat).astype(BF16)

    def gather(buf, ssem, rsem, k):
        return remote(buf.at[x], buf.at[x], ssem.at[k], rsem.at[x], xdev(k))

    for k in (2, 1, 3):
        gather(blk, s6, d6, k).start()
    loads[2].wait()
    loads[3].wait()
    for k in (1, 3, 2):
        xs = (x + k) % 4
        arrived(blk.at[xs], d6.at[xs])
    for xs in range(4):
        nrm[xs * 64 : (xs + 1) * 64] = modulate(blk[xs].astype(F32), mod[3:4], mod[4:5])
    tq = dot(nrm[...], w_t[0]).astype(BF16)
    tk = dot(nrm[...], w_t[1]).astype(BF16)
    tv = dot(nrm[...], w_t[2]).astype(BF16)
    r = lax.broadcasted_iota(jnp.int32, (256, 64), 0)
    s = lax.broadcasted_iota(jnp.int32, (256, 64), 1)
    same = r % 4 == s % 4
    for xs in range(4):
        span = slice(xs * 64, (xs + 1) * 64)
        sc = dot_t(stack_heads(tq[span], masks), tk[span]) * SCALE
        p = softmax(jnp.where(same, sc, -1e30))
        att[span] = pick_heads(dot(p, tv[span]), masks)
    pt[...] = dot(att[...], w_to[...]).astype(BF16).reshape(4, 64, D)

    def reduce_send(k):
        xd = (x + k) % 4
        return remote(pt.at[xd], r7.at[x], s7.at[k], d7.at[x], xdev(k))

    for k in (2, 1, 3):
        reduce_send(k).start()
    total = pt[x].astype(F32)
    for k in (1, 3, 2):
        xs = (x + k) % 4
        arrived(r7.at[xs], d7.at[xs])
        total = total + r7[xs].astype(F32)
    blk2[x] = (blk[x].astype(F32) + mod[5:6] * total).astype(BF16)

    for k in (2, 1, 3):
        gather(blk2, s7b, d7b, k).start()
    loads[4].wait()
    loads[5].wait()
    for k in (1, 3, 2):
        xs = (x + k) % 4
        arrived(blk2.at[xs], d7b.at[xs])
    for xs in range(4):
        nrm[xs * 64 : (xs + 1) * 64] = modulate(blk2[xs].astype(F32), mod[6:7], mod[7:8])

    def mlp_send(n, k):
        xd = (x + k) % 4
        return remote(
            pm.at[n, :, pl.ds(pl.multiple_of(xd * 256, 128), COVER)], r8.at[x, n],
            s8.at[n * 4 + k], d8.at[x * 2 + n], xdev(k),
        )

    for n in range(2):
        span = slice(n * 128, (n + 1) * 128)
        hid[span] = jax.nn.gelu(dot(nrm[span], w_up[...]), approximate=True).astype(BF16)
        pm[n] = dot(hid[span], w_dn[...]).astype(BF16)
        for k in (2, 1, 3):
            mlp_send(n, k).start()

    lanes = pl.ds(pl.multiple_of(x * 256, 128), COVER)
    gate = mod[8:9, lanes]
    parts = []
    for n in range(2):
        total = pm[n, :, lanes].astype(F32)
        for k in (1, 3, 2):
            xs = (x + k) % 4
            arrived(r8.at[xs, n], d8.at[xs * 2 + n])
            total = total + r8[xs, n].astype(F32)
        base = blk2[2 * n : 2 * n + 2, :, lanes].reshape(128, COVER).astype(F32)
        moved = pltpu.roll(base + gate * total, (COVER - 32 * x) % COVER, 1)
        parts.append(moved[:, :PART].astype(BF16))
    turn = one_hot(256, 256, lambda r: 64 * ((r % 16) // 4) + 4 * (r // 16) + r % 4)
    fin[...] = dot(turn, jnp.concatenate(parts, axis=0)).astype(BF16).reshape(16, 16, PART)

    b_me = 4 * w + zlo

    def back(kz, kc):
        zd, cd = (zlo + kz) % 4, (c + kc) % 2
        return remote(
            fin.at[pl.ds((2 * zd + cd) * 2, 2)], o_ref.at[:, pl.ds(b_me * 16, 16)],
            s9.at[kz * 2 + kc], d9.at[b_me], dev(zd, cd, zhi, 2 * c + t_me, x),
        )

    own_out = pltpu.make_async_copy(
        fin.at[pl.ds((2 * zlo + c) * 2, 2)], o_ref.at[:, pl.ds(b_me * 16, 16)], d9.at[b_me]
    )
    for kz in (3, 2, 1, 0):
        for kc in range(2):
            if kz or kc:
                back(kz, kc).start()

    @pl.when(at_home)
    def _():
        own_out.start()

    @pl.when(jnp.logical_not(at_home))
    def _():
        back(0, 0).start()

    for k in range(1, 4):
        for i in range(2):
            first_copy(i, k).wait_send()
        for n, t in enumerate((row_a, row_b)):
            spatial_send(n, t, k).wait_send()
        gather(blk, s6, d6, k).wait_send()
        reduce_send(k).wait_send()
        gather(blk2, s7b, d7b, k).wait_send()
        for n in range(2):
            mlp_send(n, k).wait_send()
    for k in range(1, 16):
        spread(k).wait_send()
    inner.wait_send()

    @pl.when(cross)
    def _():
        outer.wait_send()

    @pl.when(at_home)
    def _():
        first_copy(1 - slot, 0).wait_send()

    @pl.when(jnp.logical_not(at_home))
    def _():
        first_copy(0, 0).wait_send()
        first_copy(1, 0).wait_send()
        back(0, 0).wait_send()

    for kz in range(4):
        for kc in range(2):
            if kz or kc:
                back(kz, kc).wait_send()
    for b in range(8):
        arrived(o_ref.at[:, pl.ds(b * 16, 16)], d9.at[b])


def body(latents, modulation, spatial_qkv, spatial_out, temporal_qkv, temporal_out, mlp_up, mlp_down):
    anywhere = pl.BlockSpec(memory_space=pl.ANY)
    sem = pltpu.SemaphoreType.DMA
    vm = pltpu.VMEM
    out = pl.pallas_call(
        kernel,
        out_shape=jax.ShapeDtypeStruct((2, 128, PART), BF16),
        in_specs=[anywhere, pl.BlockSpec(memory_space=pltpu.VMEM)] + [anywhere] * 6,
        out_specs=anywhere,
        scratch_shapes=[
            vm((3, D, PART), BF16), vm((PART, D), BF16), vm((3, D, PART), BF16), vm((PART, D), BF16),
            vm((D, D), BF16), vm((D, D), BF16),
            vm((4, 2, 128, PART), BF16),
            vm((256, D), BF16),
            vm((256, D), BF16),
            vm((2, 128, PART), BF16),
            vm((2, 256, PART), BF16),
            vm((2, 128, PART), BF16),
            vm((2, 128, PART), BF16),
            vm((2, 128, D), BF16),
            vm((4, 2, 32, D), BF16),
            vm((2, 32, D), BF16),
            vm((2, 32, D), BF16),
            vm((16, 16, COVER), BF16),
            vm((16, 16, COVER), BF16),
            vm((4, 64, D), BF16),
            vm((256, PART), BF16),
            vm((4, 64, D), BF16),
            vm((4, 64, D), BF16),
            vm((4, 64, D), BF16),
            vm((256, D), BF16),
            vm((2, 128, D), BF16),
            vm((4, 2, 128, COVER), BF16),
            vm((16, 16, PART), BF16),
            sem((6,)),
            sem((8,)), sem((8,)), sem((2,)), sem((2,)), sem((8,)), sem((8,)), sem((16,)), sem((16,)),
            sem((4,)), sem((4,)), sem((4,)), sem((4,)), sem((4,)), sem((4,)), sem((8,)), sem((8,)),
            sem((8,)), sem((8,)),
        ],
        compiler_params=pltpu.CompilerParams(
            collective_id=0, has_side_effects=True, vmem_limit_bytes=48 * 2**20
        ),
        name="block",
    )(
        latents.reshape(2, 128, PART), modulation, spatial_qkv, spatial_out, temporal_qkv, temporal_out,
        mlp_up, mlp_down,
    )
    return out.reshape(latents.shape)


def solution(mesh):
    return jax.shard_map(
        body,
        mesh=mesh,
        in_specs=(
            P("tm", "height", None, "head"),
            P(),
            P(None, None, "head"),
            P("head", None),
            P(None, None, "head"),
            P("head", None),
            P(None, "head"),
            P("head", None),
        ),
        out_specs=P("tm", "height", None, "head"),
        check_vma=False,
    )
```

time: 459 us -> 101 us (0.22)
  blocking collectives: 160 us -> 0 us
  local copies, waits for them, and re-layouts: 122 us -> 9.93 us
  waiting for transfers between devices: 105 us -> 0 us
  Pallas kernels: 0 us -> 90.4 us
  starting transfers between devices: 25.2 us -> 0 us
  matrix products: 23 us -> 0 us
  between operations: 13.5 us -> 0.04 us
  other arithmetic: 5.4 us -> 0 us
    all_gather x3 -> x0, blocking collectives: 149 us -> none  [the longest x2 96.5 us: merge_branch(): full_rows = lax.all_gather(own_part, 'head', axis=3, tiled=True)]
    pallas_call x0 -> x1, Pallas kernels: none -> 90.4 us  [body(): pl.pallas_call(kernel, out_shape=jax.ShapeDtypeStruct((2, 128, PART), BF1...]
    unnamed x6 -> x0, waiting for transfers between devices: 87.8 us -> none
    unnamed x45 -> x11, local copies, waits for them, and re-layouts: 64.2 us -> 9.93 us
    another operation x8 -> x0, local copies, waits for them, and re-layouts: 28.6 us -> none
    all_to_all x3 -> x0, starting transfers between devices: 19.1 us -> none  [the longest x1 7.54 us: body(): lax.all_to_all(triple[1], 'tm', split_axis=1, concat_axis=0, tiled=True)]
    dot_general x8 -> x0, matrix products: 18.6 us -> none  [the longest x1 3.78 us: body(): jnp.dot(hidden, mlp_down, preferred_element_type=jnp.float32)]
    all_gather x3 -> x0, local copies, waits for them, and re-layouts: 14.5 us -> none  [the longest x2 9.64 us: merge_branch(): full_rows = lax.all_gather(own_part, 'head', axis=3, tiled=True)]
  transfers between devices with their start and end apart: 8 -> 0, of which waited for: 8 -> 0; matrix products, arithmetic and copies ran while one was open for 2% -> 0% of each run, Pallas kernels for 0% -> 0%
where the time goes in v1:
time: 101 us; the launch traced here: 100 us
  Pallas kernels  90.4 us (90%)
  local copies, waits for them, and re-layouts  9.93 us (10%)
    pallas_call x1, Pallas kernels, body(): pl.pallas_call(kernel, out_shape=jax.ShapeDtypeStruct((2, 128, PART), BF1...  90.4 us
    unnamed x11, local copies, waits for them, and re-layouts  9.93 us

profile of v1, /device:TPU:1, one launch (start us, length us, event | category | flops | bytes accessed | tf_op | source)
XLA Modules:
  0.0 100.4 jit_solution(409194856262715877)
XLA Ops:
  0.0 3.0 %copy.9.wqkv_h = bf16[3,1152,288]{2,1,0:T(8,128)(2,1)S(1)} copy(bf16[3,1152,288]{1,2,0:T(8,128)(2,1)} %param.10) | data formatting | bytes 3981312 | tf_op args[2]
  3.0 0.0 copy-start
  3.0 0.0 copy-start.2
  3.0 4.3 %copy.10.tqkv_h = bf16[3,1152,288]{2,1,0:T(8,128)(2,1)} copy(bf16[3,1152,288]{1,2,0:T(8,128)(2,1)} %param.12) | data formatting | bytes 3981312 | tf_op args[4]
  7.3 0.0 copy-done
  7.3 0.0 copy-done.2
  7.3 0.0 copy-start.1
  7.3 1.1 %copy-done.1 = bf16[288,1152]{1,0:T(8,128)(2,1)S(1)} copy-done((bf16[288,1152]{1,0:T(8,128)(2,1)S(1)}, bf16[288,1152]{1,0:T(8,128)(2,1)}, u32[]{:S(2)}) %copy-start.1) | copy-done | bytes 663576
  8.4 0.0 copy-start.3
  8.4 0.9 copy-done.3
  9.3 90.4 %block.1 = bf16[2,128,288]{2,1,0:T(8,128)(2,1)S(1)} custom-call(bf16[2,128,288]{2,1,0:T(8,128)(2,1)S(1)} %bitcast.3, f32[9,1152]{1,0:T(8,128)S(1)} %copy-done.3, bf16[3,1152,288]{2,1,0:T(8,128)(2,1)S(1)} %copy.9.wqkv_h, bf16[288,1152]{1,0:T(8,128)(2,1)S(1)} %copy-done, bf16[3,1152,288]{2,1,0:T(8,128)(2,1)} %copy.10.tqkv_h, bf16[288,1152]{1,0:T(8,128)(2,1)S(1)} %copy-done.1, ...), custom_call_target="tpu_custom_call" | custom-call | tf_op jit(solution)/shard_map/block/pallas_call | solution.py:408
  99.7 0.7 copy.12
Async XLA Ops:
  3.0 4.3 %copy-start = (bf16[288,1152]{1,0:T(8,128)(2,1)S(1)}, bf16[288,1152]{1,0:T(8,128)(2,1)}, u32[]{:S(2)}) copy-start(bf16[288,1152]{1,0:T(8,128)(2,1)} %wo_h.1) | copy-start | bytes 1990660
  3.0 4.3 %copy-start.2 = (bf16[2,8,16,288]{3,2,1,0:T(8,128)(2,1)S(1)}, bf16[2,8,16,288]{3,2,1,0:T(8,128)(2,1)}, u32[]{:S(2)}) copy-start(bf16[2,8,16,288]{3,2,1,0:T(8,128)(2,1)} %param.8) | copy-start | bytes 442372
  7.3 1.1 %copy-start.1 = (bf16[288,1152]{1,0:T(8,128)(2,1)S(1)}, bf16[288,1152]{1,0:T(8,128)(2,1)}, u32[]{:S(2)}) copy-start(bf16[288,1152]{1,0:T(8,128)(2,1)} %to_h.1) | copy-start | bytes 1990660
  8.4 0.9 copy-start.3

commit v2 on v1

v2 whole, which is shorter than its diff:
```python
import jax
import jax.numpy as jnp
from jax import lax
from jax.experimental import pallas as pl
from jax.experimental.pallas import tpu as pltpu
from jax.sharding import PartitionSpec as P

D = 1152
HEAD_DIM = 72
PART = 288
COVER = 384
HEADS = 4
EPSILON = 1e-06
SCALE = HEAD_DIM ** (-0.5)
MESH = pl.DeviceIdType.MESH
F32 = jnp.float32
BF16 = jnp.bfloat16
ORDER = [(0, 0), (0, 1), (1, 0), (1, 1), (2, 0), (2, 1), (3, 0), (3, 1), (4, 0), (4, 1), (5, 0), (5, 1)]


def dot(a, b):
    return jnp.dot(a, b, preferred_element_type=F32)


def dot_t(a, b):
    return lax.dot_general(a, b, (((1,), (1,)), ((), ())), preferred_element_type=F32)


def modulate(v, shift, scale):
    mean = jnp.mean(v, axis=-1, keepdims=True)
    cen = v - mean
    var = jnp.mean(cen * cen, axis=-1, keepdims=True)
    return (cen * lax.rsqrt(var + EPSILON) * (1.0 + scale) + shift).astype(BF16)


def grid(rows, cols):
    return (
        lax.broadcasted_iota(jnp.int32, (rows, cols), 0),
        lax.broadcasted_iota(jnp.int32, (rows, cols), 1),
    )


def flags(condition):
    return jnp.where(condition, 1.0, 0.0).astype(BF16)


def lane_masks(width, start):
    lane = lax.broadcasted_iota(jnp.int32, (1, width), 1)
    return [
        jnp.where((lane >= start + HEAD_DIM * h) & (lane < start + HEAD_DIM * (h + 1)), 1.0, 0.0)
        for h in range(HEADS)
    ]


def stack_heads(q, masks):
    return jnp.concatenate([(q * m).astype(BF16) for m in masks], axis=0)


def pick_heads(o, masks):
    n = o.shape[0] // HEADS
    total = o[0:n] * masks[0]
    for h in range(1, HEADS):
        total = total + o[h * n : (h + 1) * n] * masks[h]
    return total[:, PART:].astype(BF16)


def softmax(s):
    top = jnp.max(s, axis=-1, keepdims=True)
    e = jnp.exp(s - top)
    return (e / jnp.sum(e, axis=-1, keepdims=True)).astype(BF16)


def pack_part(v):
    rest = jnp.concatenate([v[32 * k : 32 * k + 32, 256:] for k in range(4)], axis=1)
    return jnp.concatenate([v[:, :128], v[:, 128:256], rest], axis=0)


def unpack_part(v):
    rest = jnp.concatenate([v[256:, 32 * k : 32 * k + 32] for k in range(4)], axis=0)
    return jnp.concatenate([v[:128], v[128:256], rest], axis=1)


def pack_kv(v):
    rest = jnp.concatenate([v[:64, 512:], v[64:, 512:]], axis=1)
    return jnp.concatenate([v[:, 128 * j : 128 * j + 128] for j in range(4)] + [rest], axis=0)


def unpack_kv(v):
    rest = jnp.concatenate([v[512:, :64], v[512:, 64:]], axis=0)
    return jnp.concatenate([v[128 * j : 128 * j + 128] for j in range(4)] + [rest], axis=1)


def kernel(
    lat, mod_h, wqkv_h, wo_h, tqkv_h, to_h, up_h, dn_h, o_ref,
    mod, w_s, w_so, w_t, w_to, w_up, w_dn, w_dp,
    lv, lp, g, lfull, qb, kvf, hp, inn, outr, ps, r4, lsel, pk, a2, blk, pt, r7, blk2, pmp, r8, fin,
    spread_sel, unpack_sel, turn,
    wsem, s1, d1, sh, dh, s4, d4, s5, d5, s6, d6, s7, d7, s7b, d7b, s8, d8, s9, d9, zsem, csem,
):
    tm = lax.axis_index("tm")
    he = lax.axis_index("height")
    x = lax.axis_index("head")
    zlo, c = tm // 2, tm % 2
    zhi, y = he // 4, he % 4
    m_me = 4 * y + zlo
    f_me = 4 * zlo + y
    at_home = y // 2 == c
    away = y // 2 != c
    cross = zhi != c
    row_a, row_b = 1 - c, c
    row_of = (row_a, row_b)

    def dev(zlo, c, zhi, y, x):
        return (zlo * 2 + c, zhi * 4 + y, x)

    def xdev(k):
        return (tm, he, (x + k) % 4)

    def group_dev(m):
        return dev(m % 4, c, zhi, m // 4, x)

    def remote(src, dst, ssem, rsem, device):
        return pltpu.make_async_remote_copy(
            src_ref=src, dst_ref=dst, send_sem=ssem, recv_sem=rsem, device_id=device, device_id_type=MESH
        )

    def arrived(dst, rsem):
        pltpu.make_async_copy(dst, dst, rsem).wait()

    sent = []

    def send(copy):
        copy.start()
        sent.append(copy.wait_send)

    def send_if(condition, copy):
        pl.when(condition)(copy.start)
        sent.append(lambda: pl.when(condition)(copy.wait_send))

    loads = [
        pltpu.make_async_copy(wqkv_h, w_s, wsem.at[0]),
        pltpu.make_async_copy(wo_h, w_so, wsem.at[1]),
        pltpu.make_async_copy(tqkv_h, w_t, wsem.at[2]),
        pltpu.make_async_copy(to_h, w_to, wsem.at[3]),
        pltpu.make_async_copy(up_h, w_up, wsem.at[4]),
        pltpu.make_async_copy(dn_h, w_dn, wsem.at[5]),
        pltpu.make_async_copy(mod_h, mod, wsem.at[6]),
        pltpu.make_async_copy(lat, lv, wsem.at[7]),
    ]
    for k in (7, 6, 0, 1, 5, 2, 3, 4):
        loads[k].start()

    bar = pltpu.get_barrier_semaphore()

    def tell(device):
        pl.semaphore_signal(bar, inc=1, device_id=device, device_id_type=MESH)

    def first_peer(i, k):
        return dev(zlo, y // 2, zhi, 2 * c + i, (x + k) % 4)

    def z_peer(k):
        return dev((zlo + k) % 4, c, zhi, y, x)

    for k in range(1, 4):
        for i in range(2):
            tell(first_peer(i, k))
    for k in range(1, 4):
        tell(xdev(k))
        tell(dev(zlo, c, zhi, (y + k) % 4, x))
        tell(z_peer(k))
    tell(dev(zlo, 1 - c, zhi, y, x))

    @pl.when(cross)
    def _():
        tell(dev(zlo, 1 - c, 1 - zhi, y, x))

    @pl.when(away)
    def _():
        for i in range(2):
            tell(first_peer(i, 0))

    loads[7].wait()
    for i in range(2):
        lp[i] = pack_part(lv[i].astype(F32)).astype(BF16)
    pl.semaphore_wait(bar, 16 + jnp.where(cross, 1, 0) + jnp.where(away, 2, 0))

    slot = y % 2

    def first_copy(i, k):
        return remote(lp.at[i], g.at[x, slot], s1.at[i * 4 + k], d1.at[x * 2 + slot], first_peer(i, k))

    for k in (2, 1, 3):
        for i in range(2):
            send(first_copy(i, k))

    @pl.when(at_home)
    def _():
        pltpu.make_async_copy(lp.at[slot], g.at[x, slot], d1.at[x * 2 + slot]).start()

    send_if(at_home, first_copy(1 - slot, 0))
    for i in range(2):
        send_if(away, first_copy(i, 0))

    for k in range(1, 4):
        pl.semaphore_signal(zsem, inc=1, device_id=z_peer(k), device_id_type=MESH)

    q_masks = lane_masks(PART, 0)
    v_masks = lane_masks(2 * PART, PART)
    r, s = grid(256, 160)
    spread_sel[...] = flags((r // 16 == (s % 32) // 2) & ((r % 16) // 2 == s // 32) & (r % 2 == s % 2))
    r, s = grid(160, 256)
    unpack_sel[...] = flags((r % 16 == s // 16) & (r // 32 == (s % 16) // 2) & ((r % 32) // 16 == s % 2))
    r, s = grid(128, 128)
    order = flags(s == 8 * ((r % 32) // 2) + 2 * (r // 32) + r % 2)
    turn[...] = flags(s == 32 * ((r % 8) // 2) + 16 * (r % 2) + r // 8)
    r, s = grid(32, 128)
    chosen = flags(s == 8 * (r // 2) + 2 * x + r % 2)

    @pl.when(jnp.logical_not(cross))
    def _():
        outr[...] = jnp.zeros_like(outr)

    loads[5].wait()

    def reorder(i, _):
        span = pl.ds(pl.multiple_of(i * 128, 128), 128)
        v = w_dn[span, :].astype(F32)
        pieces = [v[:, PART * k : PART * k + 256] for k in range(4)]
        pieces += [v[:, PART * k + 256 : PART * k + PART] for k in range(4)]
        w_dp[span, :] = jnp.concatenate(pieces, axis=1).astype(BF16)
        return 0

    lax.fori_loop(0, 9, reorder, 0)
    loads[6].wait()
    loads[0].wait()

    def prepare(t):
        for xs in range(4):
            arrived(g.at[xs, t], d1.at[xs * 2 + t])
        whole = jnp.concatenate([unpack_part(g[xs, t].astype(F32)) for xs in range(4)], axis=1)
        lfull[t] = whole.astype(BF16)
        normed = modulate(whole, mod[0:1], mod[1:2])
        kv = dot_t(normed, w_s[PART:])
        kvf[t] = kv.astype(BF16)
        hp[t] = pack_kv(kv).astype(BF16)
        return normed

    normed_b = prepare(row_b)
    outer = remote(hp.at[row_b], outr, sh.at[1], dh.at[1], dev(zlo, 1 - c, 1 - zhi, y, x))
    send_if(cross, outer)
    normed_a = prepare(row_a)
    inner = remote(hp.at[row_a], inn, sh.at[0], dh.at[0], dev(zlo, 1 - c, zhi, y, x))
    send(inner)
    for t, normed in ((row_a, normed_a), (row_b, normed_b)):
        qb[t] = dot(order, dot_t(normed, w_s[:PART]).astype(BF16)).astype(BF16)
    loads[1].wait()

    def spatial(n, extra, bias):
        q4 = stack_heads(qb[row_of[n]].astype(F32), q_masks)
        kv = kvf[...].reshape(256, 2 * PART)
        far = unpack_kv(extra[...].astype(F32)).astype(BF16)
        s_own = dot_t(q4, kv[:, :PART]) * SCALE
        s_far = dot_t(q4, far[:, :PART]) * SCALE + bias
        p = softmax(jnp.concatenate([s_own, s_far], axis=1))
        o = pick_heads(dot(p[:, :256], kv) + dot(p[:, 256:], far), v_masks)
        ps[n] = dot(o, w_so[...]).astype(BF16)
        for k in (2, 1, 3):
            send(remote(
                ps.at[n, pl.ds(((x + k) % 4) * 32, 32)], r4.at[n, x], s4.at[n * 4 + k], d4.at[n * 4 + x], xdev(k)
            ))

    arrived(inn, dh.at[0])
    spatial(0, inn, 0.0)
    for n in range(2):
        lsel[n] = dot(chosen, lfull[row_of[n]]).astype(BF16)

    @pl.when(cross)
    def _():
        arrived(outr, dh.at[1])

    spatial(1, outr, jnp.where(cross, 0.0, -1e30))
    pl.semaphore_wait(zsem, 3)

    def gather(buf, n, ssem, rsem):
        for k in (2, 1, 3):
            send(remote(buf.at[n, x], buf.at[n, x], ssem.at[n * 4 + k], rsem.at[n * 4 + x], xdev(k)))

    def others(buf, n, rsem):
        for k in (1, 3, 2):
            xs = (x + k) % 4
            arrived(buf.at[n, xs], rsem.at[n * 4 + xs])

    def summed(mine, buf, n, rsem):
        total = mine.astype(F32)
        for k in (1, 3, 2):
            xs = (x + k) % 4
            arrived(buf.at[n, xs], rsem.at[n * 4 + xs])
            total = total + buf[n, xs].astype(F32)
        return total

    def stage_spread(n):
        total = summed(ps[n, pl.ds(x * 32, 32)], r4, n, d4)
        rows = (lsel[n].astype(F32) + mod[2:3] * total).astype(BF16)
        rows = jnp.concatenate([rows, jnp.zeros((32, 128), BF16)], axis=1)
        tall = jnp.concatenate([rows[:, 256 * j : 256 * j + 256] for j in range(5)], axis=0)
        pk[n] = dot(spread_sel[...], tall).astype(BF16).reshape(16, 16, 256)
        for k in range(1, 16):
            m = (m_me + k) % 16
            send(remote(pk.at[n, m], a2.at[n, f_me], s5.at[n * 16 + k], d5.at[n * 16 + f_me], group_dev(m)))
        a2[n, f_me] = pk[n, m_me]

    def stage_gather(n):
        for k in range(1, 16):
            f = (f_me + k) % 16
            arrived(a2.at[n, f], d5.at[n * 16 + f])
        tall = dot(unpack_sel[...], a2[n].reshape(256, 256)).astype(BF16)
        wide = jnp.concatenate([tall[32 * j : 32 * j + 32] for j in range(5)], axis=1)
        blk[n, x] = wide[:, :D]
        gather(blk, n, s6, d6)

    def stage_temporal(n):
        others(blk, n, d6)
        normed = modulate(blk[n].reshape(128, D).astype(F32), mod[3:4], mod[4:5])
        q4 = stack_heads(dot_t(normed, w_t[:PART]).astype(BF16).astype(F32), q_masks)
        kv = dot_t(normed, w_t[PART:]).astype(BF16)
        r, s = grid(512, 128)
        sc = jnp.where((r % 128) // 16 == s // 16, dot_t(q4, kv[:, :PART]) * SCALE, -1e30)
        o = pick_heads(dot(softmax(sc), kv), v_masks)
        pt[n] = dot(o, w_to[...]).astype(BF16).reshape(4, 32, D)
        for k in (2, 1, 3):
            send(remote(pt.at[n, (x + k) % 4], r7.at[n, x], s7.at[n * 4 + k], d7.at[n * 4 + x], xdev(k)))

    def stage_second(n):
        total = summed(pt[n, x], r7, n, d7)
        blk2[n, x] = (blk[n, x].astype(F32) + mod[5:6] * total).astype(BF16)
        gather(blk2, n, s7b, d7b)

    def stage_mlp(n):
        others(blk2, n, d7b)
        normed = modulate(blk2[n].reshape(128, D).astype(F32), mod[6:7], mod[7:8])
        hidden = jax.nn.gelu(dot(normed, w_up[...]), approximate=True).astype(BF16)
        out = dot(hidden, w_dp[...])
        for xd in range(4):
            rest = [out[32 * k : 32 * k + 32, 1024 + 32 * xd : 1056 + 32 * xd] for k in range(4)]
            pmp[n, xd] = jnp.concatenate(
                [out[:, 256 * xd : 256 * xd + 128], out[:, 256 * xd + 128 : 256 * xd + 256],
                 jnp.concatenate(rest, axis=1)], axis=0,
            ).astype(BF16)
        for k in (2, 1, 3):
            send(remote(pmp.at[n, (x + k) % 4], r8.at[n, x], s8.at[n * 4 + k], d8.at[n * 4 + x], xdev(k)))

    def stage_return(n):
        lanes = pl.ds(pl.multiple_of(x * 256, 128), COVER)
        shift = (COVER - 32 * x) % COVER
        gate = pltpu.roll(jnp.broadcast_to(mod[8:9, lanes], (8, COVER)), shift, 1)[:1, :PART]
        base = pltpu.roll(blk2[n, :, :, lanes].reshape(128, COVER).astype(F32), shift, 1)[:, :PART]
        total = unpack_part(summed(pmp[n, x], r8, n, d8))
        out = (base + gate * total).astype(BF16)
        fin[n] = dot(turn[...], out).astype(BF16).reshape(8, 16, PART)
        y_to = 2 * c + row_of[n]

        def back(kz, kc):
            zd, cd = (zlo + kz) % 4, (c + kc) % 2
            return remote(
                fin.at[n, 2 * zd + cd], o_ref.at[m_me], s9.at[n * 8 + kz * 2 + kc], d9.at[m_me], dev(zd, cd, zhi, y_to, x)
            )

        for kz in (3, 2, 1, 0):
            for kc in range(2):
                if kz or kc:
                    send(back(kz, kc))
        here = y_to == y
        send_if(jnp.logical_not(here), back(0, 0))

        @pl.when(here)
        def _():
            pltpu.make_async_copy(fin.at[n, 2 * zlo + c], o_ref.at[m_me], d9.at[m_me]).start()

    for k in (2, 3, 4):
        loads[k].wait()
    stages = (stage_spread, stage_gather, stage_temporal, stage_second, stage_mlp, stage_return)
    for k, n in ORDER:
        stages[k](n)
        if (k, n) == (1, 1):
            pl.semaphore_signal(csem, inc=1, device_id=dev(zlo, 1 - c, zhi, y, x), device_id_type=MESH)
        if (k, n) == (4, 0):
            pl.semaphore_wait(csem, 1)

    for done in sent:
        done()
    for m in range(16):
        arrived(o_ref.at[m], d9.at[m])


def body(latents, modulation, spatial_qkv, spatial_out, temporal_qkv, temporal_out, mlp_up, mlp_down):
    anywhere = pl.BlockSpec(memory_space=pl.ANY)
    sem = pltpu.SemaphoreType.DMA

    def vm(*shape):
        return pltpu.VMEM(shape, BF16)

    out = pl.pallas_call(
        kernel,
        out_shape=jax.ShapeDtypeStruct((16, 16, PART), BF16),
        in_specs=[anywhere] * 8,
        out_specs=anywhere,
        scratch_shapes=[
            pltpu.VMEM((9, D), F32),
            vm(3 * PART, D), vm(PART, D), vm(3 * PART, D), vm(PART, D), vm(D, D), vm(D, D), vm(D, D),
            vm(2, 128, PART),
            vm(2, PART, 128),
            vm(4, 2, PART, 128),
            vm(2, 128, D),
            vm(2, 128, PART),
            vm(2, 128, 2 * PART),
            vm(2, 2 * PART, 128),
            vm(2 * PART, 128),
            vm(2 * PART, 128),
            vm(2, 128, D),
            vm(2, 4, 32, D),
            vm(2, 32, D),
            vm(2, 16, 16, 256),
            vm(2, 16, 16, 256),
            vm(2, 4, 32, D),
            vm(2, 4, 32, D),
            vm(2, 4, 32, D),
            vm(2, 4, 32, D),
            vm(2, 4, PART, 128),
            vm(2, 4, PART, 128),
            vm(2, 8, 16, PART),
            vm(256, 160), vm(160, 256), vm(128, 128),
            sem((8,)),
            sem((8,)), sem((8,)), sem((2,)), sem((2,)), sem((8,)), sem((8,)), sem((32,)), sem((32,)),
            sem((8,)), sem((8,)), sem((8,)), sem((8,)), sem((8,)), sem((8,)), sem((8,)), sem((8,)),
            sem((16,)), sem((16,)),
            pltpu.SemaphoreType.REGULAR, pltpu.SemaphoreType.REGULAR,
        ],
        compiler_params=pltpu.CompilerParams(
            collective_id=0, has_side_effects=True, vmem_limit_bytes=60 * 2**20
        ),
        name="block",
    )(
        latents.reshape(2, 128, PART), modulation,
        jnp.swapaxes(spatial_qkv, 1, 2).reshape(3 * PART, D), spatial_out,
        jnp.swapaxes(temporal_qkv, 1, 2).reshape(3 * PART, D), temporal_out, mlp_up, mlp_down,
    )
    return out.reshape(16, 2, 8, PART).transpose(1, 0, 2, 3).reshape(latents.shape)


def solution(mesh):
    return jax.shard_map(
        body,
        mesh=mesh,
        in_specs=(
            P("tm", "height", None, "head"),
            P(),
            P(None, None, "head"),
            P("head", None),
            P(None, None, "head"),
            P("head", None),
            P(None, "head"),
            P("head", None),
        ),
        out_specs=P("tm", "height", None, "head"),
        check_vma=False,
    )
```

time: 101 us -> 75.5 us (0.75)
  Pallas kernels: 90.4 us -> 73.7 us
  local copies, waits for them, and re-layouts: 9.93 us -> 1.62 us
    pallas_call x1, Pallas kernels: 90.4 us -> 73.7 us  [body(): pl.pallas_call(kernel, out_shape=jax.ShapeDtypeStruct((16, 16, PART), BF1...]
    unnamed x11 -> x0, local copies, waits for them, and re-layouts: 9.93 us -> none
    transpose x0 -> x1, local copies, waits for them, and re-layouts: none -> 1.62 us  [body(): out.reshape(16, 2, 8, PART).transpose(1, 0, 2, 3).reshape(latents.shape)]
where the time goes in v2:
time: 75.5 us; the launch traced here: 75.4 us
  Pallas kernels  73.7 us (98%)
  local copies, waits for them, and re-layouts  1.62 us (2%)
    pallas_call x1, Pallas kernels, body(): pl.pallas_call(kernel, out_shape=jax.ShapeDtypeStruct((16, 16, PART), BF1...  73.7 us
    transpose x1, local copies, waits for them, and re-layouts, body(): out.reshape(16, 2, 8, PART).transpose(1, 0, 2, 3).reshape(latents.shape)  1.62 us

profile of v2, /device:TPU:1, one launch (start us, length us, event | category | flops | bytes accessed | tf_op | source)
XLA Modules:
  0.0 75.4 jit_solution(9686062972512361348)
XLA Ops:
  0.0 73.7 %block.1 = bf16[16,16,288]{2,1,0:T(8,128)(2,1)} custom-call(bf16[2,128,288]{2,1,0:T(8,128)(2,1)} %bitcast.14, f32[9,1152]{1,0:T(8,128)} %mod_h.1, bf16[864,1152]{1,0:T(8,128)(2,1)} %bitcast.11, bf16[288,1152]{1,0:T(8,128)(2,1)} %wo_h.1, bf16[864,1152]{1,0:T(8,128)(2,1)} %bitcast.12, bf16[288,1152]{1,0:T(8,128)(2,1)} %to_h.1, bf16[1152,1152]{1,0:T(8,128)(2,1)} %up_h.1, ...), custom_call_target="tpu_custom_call" | custom-call | tf_op jit(solution)/shard_map/block/pallas_call | solution.py:402
  73.7 1.6 %copy.9 = bf16[2,16,8,288]{3,2,1,0:T(8,128)(2,1)} copy(bf16[2,16,8,288]{3,2,0,1:T(8,128)(2,1)} %bitcast.13) | data formatting | bytes 294912 | tf_op jit(solution)/shard_map/transpose | solution.py:447

commit v3 on v2

--- a/solution.py
+++ b/solution.py
@@ -15,7 +15,9 @@
 MESH = pl.DeviceIdType.MESH
 F32 = jnp.float32
 BF16 = jnp.bfloat16
-ORDER = [(0, 0), (0, 1), (1, 0), (1, 1), (2, 0), (2, 1), (3, 0), (3, 1), (4, 0), (4, 1), (5, 0), (5, 1)]
+CUT = 1
+RUN = 32 // CUT
+ORDER = [(k, n, 0) for k in range(6) for n in range(2)]
 
 
 def dot(a, b):
@@ -92,10 +94,10 @@
 
 def kernel(
     lat, mod_h, wqkv_h, wo_h, tqkv_h, to_h, up_h, dn_h, o_ref,
-    mod, w_s, w_so, w_t, w_to, w_up, w_dn, w_dp,
+    mod, w_s, w_so, w_t, w_to, w_up, w_dn, w_dp, c_s, c_t,
     lv, lp, g, lfull, qb, kvf, hp, inn, outr, ps, r4, lsel, pk, a2, blk, pt, r7, blk2, pmp, r8, fin,
     spread_sel, unpack_sel, turn,
-    wsem, s1, d1, sh, dh, s4, d4, s5, d5, s6, d6, s7, d7, s7b, d7b, s8, d8, s9, d9, zsem, csem,
+    wsem, s1, d1, sh, dh, s4, d4, s5, d5, s6, d6, s7, d7, s7b, d7b, s8, d8, s9, d9, zsem, ysem, xsem, csem,
 ):
     tm = lax.axis_index("tm")
     he = lax.axis_index("height")
@@ -158,8 +160,11 @@
     def first_peer(i, k):
         return dev(zlo, y // 2, zhi, 2 * c + i, (x + k) % 4)
 
-    def z_peer(k):
-        return dev((zlo + k) % 4, c, zhi, y, x)
+    z_near = zlo + 1 - 2 * (zlo % 2)
+    z_far = (3 - zlo, (zlo + 2) % 4, z_near, zlo)
+
+    def z_dev(z):
+        return dev(z, c, zhi, y, x)
 
     for k in range(1, 4):
         for i in range(2):
@@ -167,12 +172,12 @@
     for k in range(1, 4):
         tell(xdev(k))
         tell(dev(zlo, c, zhi, (y + k) % 4, x))
-        tell(z_peer(k))
     tell(dev(zlo, 1 - c, zhi, y, x))
 
-    @pl.when(cross)
-    def _():
-        tell(dev(zlo, 1 - c, 1 - zhi, y, x))
+    for k in range(1, 4):
+        pl.when(zlo + k < 4)(lambda k=k: tell(z_dev(zlo + k)))
+    cross_dev = dev(zlo, 1 - c, 1 - zhi, y, x)
+    pl.when(cross & (zhi == 0))(lambda: tell(cross_dev))
 
     @pl.when(away)
     def _():
@@ -182,7 +187,7 @@
     loads[7].wait()
     for i in range(2):
         lp[i] = pack_part(lv[i].astype(F32)).astype(BF16)
-    pl.semaphore_wait(bar, 16 + jnp.where(cross, 1, 0) + jnp.where(away, 2, 0))
+    pl.semaphore_wait(bar, 13 + zlo + jnp.where(cross & (zhi == 1), 1, 0) + jnp.where(away, 2, 0))
 
     slot = y % 2
 
@@ -201,8 +206,12 @@
     for i in range(2):
         send_if(away, first_copy(i, 0))
 
+    def answer(semaphore, device):
+        pl.semaphore_signal(semaphore, inc=1, device_id=device, device_id_type=MESH)
+
     for k in range(1, 4):
-        pl.semaphore_signal(zsem, inc=1, device_id=z_peer(k), device_id_type=MESH)
+        pl.when(zlo >= k)(lambda k=k: answer(zsem, z_dev(zlo - k)))
+    pl.when(cross & (zhi == 1))(lambda: answer(xsem, cross_dev))
 
     q_masks = lane_masks(PART, 0)
     v_masks = lane_masks(2 * PART, PART)
@@ -212,7 +221,10 @@
     unpack_sel[...] = flags((r % 16 == s // 16) & (r // 32 == (s % 16) // 2) & ((r % 32) // 16 == s % 2))
     r, s = grid(128, 128)
     order = flags(s == 8 * ((r % 32) // 2) + 2 * (r // 32) + r % 2)
-    turn[...] = flags(s == 32 * ((r % 8) // 2) + 16 * (r % 2) + r // 8)
+    if CUT == 1:
+        turn[...] = flags(s == 32 * ((r % 8) // 2) + 16 * (r % 2) + r // 8)
+    else:
+        turn[...] = flags(s == 64 * (r % 2) + 16 * ((r % 8) // 2) + r // 8)
     r, s = grid(32, 128)
     chosen = flags(s == 8 * (r // 2) + 2 * x + r % 2)
 
@@ -232,7 +244,21 @@
 
     lax.fori_loop(0, 9, reorder, 0)
     loads[6].wait()
+
+    def turn_over(source, target):
+        def step(i, _):
+            span = pl.ds(pl.multiple_of(i * 128, 128), 128)
+            v = source[:, span].astype(F32)
+            v = jnp.concatenate([v[PART:], v[:PART]], axis=0)
+            target[span, :] = v.T.astype(BF16)
+            return 0
+
+        lax.fori_loop(0, 9, step, 0)
+
     loads[0].wait()
+    turn_over(w_s, c_s)
+    loads[2].wait()
+    turn_over(w_t, c_t)
 
     def prepare(t):
         for xs in range(4):
@@ -240,19 +266,20 @@
         whole = jnp.concatenate([unpack_part(g[xs, t].astype(F32)) for xs in range(4)], axis=1)
         lfull[t] = whole.astype(BF16)
         normed = modulate(whole, mod[0:1], mod[1:2])
-        kv = dot_t(normed, w_s[PART:])
+        kv = dot(normed, c_s[:, : 2 * PART])
         kvf[t] = kv.astype(BF16)
         hp[t] = pack_kv(kv).astype(BF16)
         return normed
 
     normed_b = prepare(row_b)
-    outer = remote(hp.at[row_b], outr, sh.at[1], dh.at[1], dev(zlo, 1 - c, 1 - zhi, y, x))
+    pl.when(cross & (zhi == 0))(lambda: pl.semaphore_wait(xsem, 1))
+    outer = remote(hp.at[row_b], outr, sh.at[1], dh.at[1], cross_dev)
     send_if(cross, outer)
     normed_a = prepare(row_a)
     inner = remote(hp.at[row_a], inn, sh.at[0], dh.at[0], dev(zlo, 1 - c, zhi, y, x))
     send(inner)
     for t, normed in ((row_a, normed_a), (row_b, normed_b)):
-        qb[t] = dot(order, dot_t(normed, w_s[:PART]).astype(BF16)).astype(BF16)
+        qb[t] = dot(order, dot(normed, c_s[:, 2 * PART :]).astype(BF16)).astype(BF16)
     loads[1].wait()
 
     def spatial(n, extra, bias):
@@ -269,6 +296,9 @@
                 ps.at[n, pl.ds(((x + k) % 4) * 32, 32)], r4.at[n, x], s4.at[n * 4 + k], d4.at[n * 4 + x], xdev(k)
             ))
 
+    pl.when(zlo < 3)(lambda: pl.semaphore_wait(zsem, 3 - zlo))
+    for k in range(1, 4):
+        pl.when(zlo + k < 4)(lambda k=k: answer(ysem, z_dev(zlo + k)))
     arrived(inn, dh.at[0])
     spatial(0, inn, 0.0)
     for n in range(2):
@@ -279,65 +309,74 @@
         arrived(outr, dh.at[1])
 
     spatial(1, outr, jnp.where(cross, 0.0, -1e30))
-    pl.semaphore_wait(zsem, 3)
-
-    def gather(buf, n, ssem, rsem):
+    pl.when(zlo > 0)(lambda: pl.semaphore_wait(ysem, zlo))
+
+    def gather(buf, i, ssem, rsem):
         for k in (2, 1, 3):
-            send(remote(buf.at[n, x], buf.at[n, x], ssem.at[n * 4 + k], rsem.at[n * 4 + x], xdev(k)))
-
-    def others(buf, n, rsem):
+            send(remote(buf.at[i, x], buf.at[i, x], ssem.at[i * 4 + k], rsem.at[i * 4 + x], xdev(k)))
+
+    def others(buf, i, rsem):
         for k in (1, 3, 2):
             xs = (x + k) % 4
-            arrived(buf.at[n, xs], rsem.at[n * 4 + xs])
-
-    def summed(mine, buf, n, rsem):
+            arrived(buf.at[i, xs], rsem.at[i * 4 + xs])
+
+    def summed(mine, buf, i, rsem):
         total = mine.astype(F32)
         for k in (1, 3, 2):
             xs = (x + k) % 4
-            arrived(buf.at[n, xs], rsem.at[n * 4 + xs])
-            total = total + buf[n, xs].astype(F32)
+            arrived(buf.at[i, xs], rsem.at[i * 4 + xs])
+            total = total + buf[i, xs].astype(F32)
         return total
 
-    def stage_spread(n):
+    def stage_spread(n, u):
         total = summed(ps[n, pl.ds(x * 32, 32)], r4, n, d4)
         rows = (lsel[n].astype(F32) + mod[2:3] * total).astype(BF16)
         rows = jnp.concatenate([rows, jnp.zeros((32, 128), BF16)], axis=1)
         tall = jnp.concatenate([rows[:, 256 * j : 256 * j + 256] for j in range(5)], axis=0)
         pk[n] = dot(spread_sel[...], tall).astype(BF16).reshape(16, 16, 256)
-        for k in range(1, 16):
-            m = (m_me + k) % 16
-            send(remote(pk.at[n, m], a2.at[n, f_me], s5.at[n * 16 + k], d5.at[n * 16 + f_me], group_dev(m)))
+        for j in range(4):
+            for k in (2, 1, 3, 0):
+                if j < 3 or k:
+                    m = 4 * ((y + k) % 4) + z_far[j]
+                    send(remote(
+                        pk.at[n, m], a2.at[n, f_me], s5.at[n * 16 + 4 * j + k], d5.at[n * 16 + f_me], group_dev(m)
+                    ))
         a2[n, f_me] = pk[n, m_me]
 
-    def stage_gather(n):
+    def stage_gather(n, u):
         for k in range(1, 16):
             f = (f_me + k) % 16
             arrived(a2.at[n, f], d5.at[n * 16 + f])
         tall = dot(unpack_sel[...], a2[n].reshape(256, 256)).astype(BF16)
         wide = jnp.concatenate([tall[32 * j : 32 * j + 32] for j in range(5)], axis=1)
-        blk[n, x] = wide[:, :D]
-        gather(blk, n, s6, d6)
-
-    def stage_temporal(n):
-        others(blk, n, d6)
-        normed = modulate(blk[n].reshape(128, D).astype(F32), mod[3:4], mod[4:5])
-        q4 = stack_heads(dot_t(normed, w_t[:PART]).astype(BF16).astype(F32), q_masks)
-        kv = dot_t(normed, w_t[PART:]).astype(BF16)
-        r, s = grid(512, 128)
-        sc = jnp.where((r % 128) // 16 == s // 16, dot_t(q4, kv[:, :PART]) * SCALE, -1e30)
+        for v in range(CUT):
+            blk[n * CUT + v, x] = wide[v * RUN : (v + 1) * RUN, :D]
+            gather(blk, n * CUT + v, s6, d6)
+
+    def stage_temporal(n, u):
+        i = n * CUT + u
+        others(blk, i, d6)
+        normed = modulate(blk[i].reshape(4 * RUN, D).astype(F32), mod[3:4], mod[4:5])
+        qkv = dot(normed, c_t[...])
+        q4 = stack_heads(qkv[:, 2 * PART :].astype(BF16).astype(F32), q_masks)
+        kv = qkv[:, : 2 * PART].astype(BF16)
+        r, s = grid(16 * RUN, 4 * RUN)
+        sc = jnp.where((r % (4 * RUN)) // 16 == s // 16, dot_t(q4, kv[:, :PART]) * SCALE, -1e30)
         o = pick_heads(dot(softmax(sc), kv), v_masks)
-        pt[n] = dot(o, w_to[...]).astype(BF16).reshape(4, 32, D)
+        pt[i] = dot(o, w_to[...]).astype(BF16).reshape(4, RUN, D)
         for k in (2, 1, 3):
-            send(remote(pt.at[n, (x + k) % 4], r7.at[n, x], s7.at[n * 4 + k], d7.at[n * 4 + x], xdev(k)))
-
-    def stage_second(n):
-        total = summed(pt[n, x], r7, n, d7)
-        blk2[n, x] = (blk[n, x].astype(F32) + mod[5:6] * total).astype(BF16)
-        gather(blk2, n, s7b, d7b)
-
-    def stage_mlp(n):
-        others(blk2, n, d7b)
-        normed = modulate(blk2[n].reshape(128, D).astype(F32), mod[6:7], mod[7:8])
+            send(remote(pt.at[i, (x + k) % 4], r7.at[i, x], s7.at[i * 4 + k], d7.at[i * 4 + x], xdev(k)))
+
+    def stage_second(n, u):
+        i = n * CUT + u
+        total = summed(pt[i, x], r7, i, d7)
+        blk2[i, x] = (blk[i, x].astype(F32) + mod[5:6] * total).astype(BF16)
+        gather(blk2, i, s7b, d7b)
+
+    def stage_mlp(n, u):
+        for v in range(CUT):
+            others(blk2, n * CUT + v, d7b)
+        normed = modulate(blk2[n * CUT : (n + 1) * CUT].reshape(128, D).astype(F32), mod[6:7], mod[7:8])
         hidden = jax.nn.gelu(dot(normed, w_up[...]), approximate=True).astype(BF16)
         out = dot(hidden, w_dp[...])
         for xd in range(4):
@@ -349,38 +388,38 @@
         for k in (2, 1, 3):
             send(remote(pmp.at[n, (x + k) % 4], r8.at[n, x], s8.at[n * 4 + k], d8.at[n * 4 + x], xdev(k)))
 
-    def stage_return(n):
+    def stage_return(n, u):
         lanes = pl.ds(pl.multiple_of(x * 256, 128), COVER)
         shift = (COVER - 32 * x) % COVER
         gate = pltpu.roll(jnp.broadcast_to(mod[8:9, lanes], (8, COVER)), shift, 1)[:1, :PART]
-        base = pltpu.roll(blk2[n, :, :, lanes].reshape(128, COVER).astype(F32), shift, 1)[:, :PART]
+        base = pltpu.roll(blk2[n * CUT : (n + 1) * CUT, :, :, lanes].reshape(128, COVER).astype(F32), shift, 1)[:, :PART]
         total = unpack_part(summed(pmp[n, x], r8, n, d8))
         out = (base + gate * total).astype(BF16)
         fin[n] = dot(turn[...], out).astype(BF16).reshape(8, 16, PART)
         y_to = 2 * c + row_of[n]
 
-        def back(kz, kc):
-            zd, cd = (zlo + kz) % 4, (c + kc) % 2
+        def back(j, kc):
+            zd, cd = z_far[j], (c + kc) % 2
             return remote(
-                fin.at[n, 2 * zd + cd], o_ref.at[m_me], s9.at[n * 8 + kz * 2 + kc], d9.at[m_me], dev(zd, cd, zhi, y_to, x)
+                fin.at[n, 2 * zd + cd], o_ref.at[m_me], s9.at[n * 8 + j * 2 + kc], d9.at[m_me], dev(zd, cd, zhi, y_to, x)
             )
 
-        for kz in (3, 2, 1, 0):
+        for j in range(4):
             for kc in range(2):
-                if kz or kc:
-                    send(back(kz, kc))
+                if j < 3 or kc:
+                    send(back(j, kc))
         here = y_to == y
-        send_if(jnp.logical_not(here), back(0, 0))
+        send_if(jnp.logical_not(here), back(3, 0))
 
         @pl.when(here)
         def _():
             pltpu.make_async_copy(fin.at[n, 2 * zlo + c], o_ref.at[m_me], d9.at[m_me]).start()
 
-    for k in (2, 3, 4):
+    for k in (3, 4):
         loads[k].wait()
     stages = (stage_spread, stage_gather, stage_temporal, stage_second, stage_mlp, stage_return)
-    for k, n in ORDER:
-        stages[k](n)
+    for k, n, u in ORDER:
+        stages[k](n, u)
         if (k, n) == (1, 1):
             pl.semaphore_signal(csem, inc=1, device_id=dev(zlo, 1 - c, zhi, y, x), device_id_type=MESH)
         if (k, n) == (4, 0):
@@ -401,12 +440,13 @@
 
     out = pl.pallas_call(
         kernel,
-        out_shape=jax.ShapeDtypeStruct((16, 16, PART), BF16),
+        out_shape=pltpu.VMEM((16, 16, PART), BF16),
         in_specs=[anywhere] * 8,
         out_specs=anywhere,
         scratch_shapes=[
             pltpu.VMEM((9, D), F32),
             vm(3 * PART, D), vm(PART, D), vm(3 * PART, D), vm(PART, D), vm(D, D), vm(D, D), vm(D, D),
+            vm(D, 3 * PART), vm(D, 3 * PART),
             vm(2, 128, PART),
             vm(2, PART, 128),
             vm(4, 2, PART, 128),
@@ -421,18 +461,19 @@
             vm(2, 32, D),
             vm(2, 16, 16, 256),
             vm(2, 16, 16, 256),
-            vm(2, 4, 32, D),
-            vm(2, 4, 32, D),
-            vm(2, 4, 32, D),
-            vm(2, 4, 32, D),
+            vm(2 * CUT, 4, RUN, D),
+            vm(2 * CUT, 4, RUN, D),
+            vm(2 * CUT, 4, RUN, D),
+            vm(2 * CUT, 4, RUN, D),
             vm(2, 4, PART, 128),
             vm(2, 4, PART, 128),
             vm(2, 8, 16, PART),
             vm(256, 160), vm(160, 256), vm(128, 128),
             sem((8,)),
             sem((8,)), sem((8,)), sem((2,)), sem((2,)), sem((8,)), sem((8,)), sem((32,)), sem((32,)),
-            sem((8,)), sem((8,)), sem((8,)), sem((8,)), sem((8,)), sem((8,)), sem((8,)), sem((8,)),
-            sem((16,)), sem((16,)),
+            sem((8 * CUT,)), sem((8 * CUT,)), sem((8 * CUT,)), sem((8 * CUT,)), sem((8 * CUT,)), sem((8 * CUT,)),
+            sem((8,)), sem((8,)), sem((16,)), sem((16,)),
+            pltpu.SemaphoreType.REGULAR, pltpu.SemaphoreType.REGULAR,
             pltpu.SemaphoreType.REGULAR, pltpu.SemaphoreType.REGULAR,
         ],
         compiler_params=pltpu.CompilerParams(

time: 75.5 us -> 71.9 us (0.952)
  Pallas kernels: 73.7 us -> 71.1 us
  local copies, waits for them, and re-layouts: 1.62 us -> 0.7 us
    pallas_call x1, Pallas kernels: 73.7 us -> 71.1 us  [body(): pl.pallas_call(kernel, out_shape=pltpu.VMEM((16, 16, PART), BF16), in_spe...]
    transpose x1, local copies, waits for them, and re-layouts: 1.62 us -> 0.7 us  [body(): out.reshape(16, 2, 8, PART).transpose(1, 0, 2, 3).reshape(latents.shape)]
where the time goes in v3:
time: 71.9 us; the launch traced here: 71.8 us
  Pallas kernels  71.1 us (99%)
    pallas_call x1, Pallas kernels, body(): pl.pallas_call(kernel, out_shape=pltpu.VMEM((16, 16, PART), BF16), in_spe...  71.1 us

profile of v3, /device:TPU:1, one launch (start us, length us, event | category | flops | bytes accessed | tf_op | source)
XLA Modules:
  0.0 71.8 jit_solution(16699813334787337266)
XLA Ops:
  0.0 71.1 %block.1 = bf16[16,16,288]{2,1,0:T(8,128)(2,1)S(1)} custom-call(bf16[2,128,288]{2,1,0:T(8,128)(2,1)} %bitcast.14, f32[9,1152]{1,0:T(8,128)} %mod_h.1, bf16[864,1152]{1,0:T(8,128)(2,1)} %bitcast.12, bf16[288,1152]{1,0:T(8,128)(2,1)} %wo_h.1, bf16[864,1152]{1,0:T(8,128)(2,1)} %bitcast.13, bf16[288,1152]{1,0:T(8,128)(2,1)} %to_h.1, bf16[1152,1152]{1,0:T(8,128)(2,1)} %up_h.1, ...), custom_call_target="tpu_custom_call" | custom-call | tf_op jit(solution)/shard_map/block/pallas_call | solution.py:441
  71.1 0.7 copy.9

commit v4 on v3

--- a/solution.py
+++ b/solution.py
@@ -95,7 +95,7 @@
 def kernel(
     lat, mod_h, wqkv_h, wo_h, tqkv_h, to_h, up_h, dn_h, o_ref,
     mod, w_s, w_so, w_t, w_to, w_up, w_dn, w_dp, c_s, c_t,
-    lv, lp, g, lfull, qb, kvf, hp, inn, outr, ps, r4, lsel, pk, a2, blk, pt, r7, blk2, pmp, r8, fin,
+    lv, lp, g, lfull, qb, kvf, hp, halo, ps, r4, lsel, pk, a2, blk, pt, r7, blk2, pmp, r8, fin,
     spread_sel, unpack_sel, turn,
     wsem, s1, d1, sh, dh, s4, d4, s5, d5, s6, d6, s7, d7, s7b, d7b, s8, d8, s9, d9, zsem, ysem, xsem, csem,
 ):
@@ -110,7 +110,8 @@
     away = y // 2 != c
     cross = zhi != c
     row_a, row_b = 1 - c, c
-    row_of = (row_a, row_b)
+    row_of = (jnp.where(cross, row_a, row_b), jnp.where(cross, row_b, row_a))
+    halo_of = (jnp.where(cross, 0, 1), jnp.where(cross, 1, 0))
 
     def dev(zlo, c, zhi, y, x):
         return (zlo * 2 + c, zhi * 4 + y, x)
@@ -149,8 +150,7 @@
         pltpu.make_async_copy(mod_h, mod, wsem.at[6]),
         pltpu.make_async_copy(lat, lv, wsem.at[7]),
     ]
-    for k in (7, 6, 0, 1, 5, 2, 3, 4):
-        loads[k].start()
+    loads[7].start()
 
     bar = pltpu.get_barrier_semaphore()
 
@@ -184,6 +184,9 @@
         for i in range(2):
             tell(first_peer(i, 0))
 
+    for k in (6, 0, 5, 2, 1, 3, 4):
+        loads[k].start()
+
     loads[7].wait()
     for i in range(2):
         lp[i] = pack_part(lv[i].astype(F32)).astype(BF16)
@@ -194,7 +197,7 @@
     def first_copy(i, k):
         return remote(lp.at[i], g.at[x, slot], s1.at[i * 4 + k], d1.at[x * 2 + slot], first_peer(i, k))
 
-    for k in (2, 1, 3):
+    for k in (1, 3, 2):
         for i in range(2):
             send(first_copy(i, k))
 
@@ -230,7 +233,7 @@
 
     @pl.when(jnp.logical_not(cross))
     def _():
-        outr[...] = jnp.zeros_like(outr)
+        halo[1] = jnp.zeros((2 * PART, 128), BF16)
 
     loads[5].wait()
 
@@ -271,21 +274,23 @@
         hp[t] = pack_kv(kv).astype(BF16)
         return normed
 
-    normed_b = prepare(row_b)
+    first, second = row_of[1], row_of[0]
+    normed_first = prepare(first)
     pl.when(cross & (zhi == 0))(lambda: pl.semaphore_wait(xsem, 1))
-    outer = remote(hp.at[row_b], outr, sh.at[1], dh.at[1], cross_dev)
+    outer = remote(hp.at[row_b], halo.at[1], sh.at[1], dh.at[1], cross_dev)
+    inner = remote(hp.at[row_a], halo.at[0], sh.at[0], dh.at[0], dev(zlo, 1 - c, zhi, y, x))
     send_if(cross, outer)
-    normed_a = prepare(row_a)
-    inner = remote(hp.at[row_a], inn, sh.at[0], dh.at[0], dev(zlo, 1 - c, zhi, y, x))
-    send(inner)
-    for t, normed in ((row_a, normed_a), (row_b, normed_b)):
+    send_if(jnp.logical_not(cross), inner)
+    normed_second = prepare(second)
+    send_if(cross, inner)
+    for t, normed in ((second, normed_second), (first, normed_first)):
         qb[t] = dot(order, dot(normed, c_s[:, 2 * PART :]).astype(BF16)).astype(BF16)
     loads[1].wait()
 
-    def spatial(n, extra, bias):
+    def spatial(n, bias):
         q4 = stack_heads(qb[row_of[n]].astype(F32), q_masks)
         kv = kvf[...].reshape(256, 2 * PART)
-        far = unpack_kv(extra[...].astype(F32)).astype(BF16)
+        far = unpack_kv(halo[halo_of[n]].astype(F32)).astype(BF16)
         s_own = dot_t(q4, kv[:, :PART]) * SCALE
         s_far = dot_t(q4, far[:, :PART]) * SCALE + bias
         p = softmax(jnp.concatenate([s_own, s_far], axis=1))
@@ -299,16 +304,14 @@
     pl.when(zlo < 3)(lambda: pl.semaphore_wait(zsem, 3 - zlo))
     for k in range(1, 4):
         pl.when(zlo + k < 4)(lambda k=k: answer(ysem, z_dev(zlo + k)))
-    arrived(inn, dh.at[0])
-    spatial(0, inn, 0.0)
+    pl.when(cross)(lambda: arrived(halo.at[0], dh.at[0]))
+    spatial(0, jnp.where(cross, 0.0, -1e30))
     for n in range(2):
         lsel[n] = dot(chosen, lfull[row_of[n]]).astype(BF16)
 
-    @pl.when(cross)
-    def _():
-        arrived(outr, dh.at[1])
-
-    spatial(1, outr, jnp.where(cross, 0.0, -1e30))
+    pl.when(cross)(lambda: arrived(halo.at[1], dh.at[1]))
+    pl.when(jnp.logical_not(cross))(lambda: arrived(halo.at[0], dh.at[0]))
+    spatial(1, 0.0)
     pl.when(zlo > 0)(lambda: pl.semaphore_wait(ysem, zlo))
 
     def gather(buf, i, ssem, rsem):
@@ -454,8 +457,7 @@
             vm(2, 128, PART),
             vm(2, 128, 2 * PART),
             vm(2, 2 * PART, 128),
-            vm(2 * PART, 128),
-            vm(2 * PART, 128),
+            vm(2, 2 * PART, 128),
             vm(2, 128, D),
             vm(2, 4, 32, D),
             vm(2, 32, D),

time: 71.9 us -> 69.6 us (0.968)
  the two profiles are of different devices: /device:TPU:1 before, /device:TPU:9 now
where the time goes in v4:
time: 69.6 us; the launch traced here: 69.5 us
  Pallas kernels  68.8 us (99%)
  local copies, waits for them, and re-layouts  0.7 us (1%)
    pallas_call x1, Pallas kernels, body(): pl.pallas_call(kernel, out_shape=pltpu.VMEM((16, 16, PART), BF16), in_spe...  68.8 us

profile of v4, /device:TPU:9, one launch (start us, length us, event | category | flops | bytes accessed | tf_op | source)
XLA Modules:
  0.0 69.5 jit_solution(9639253964408010399)
XLA Ops:
  0.0 68.8 %block.1 = bf16[16,16,288]{2,1,0:T(8,128)(2,1)S(1)} custom-call(bf16[2,128,288]{2,1,0:T(8,128)(2,1)} %bitcast.14, f32[9,1152]{1,0:T(8,128)} %mod_h.1, bf16[864,1152]{1,0:T(8,128)(2,1)} %bitcast.12, bf16[288,1152]{1,0:T(8,128)(2,1)} %wo_h.1, bf16[864,1152]{1,0:T(8,128)(2,1)} %bitcast.13, bf16[288,1152]{1,0:T(8,128)(2,1)} %to_h.1, bf16[1152,1152]{1,0:T(8,128)(2,1)} %up_h.1, ...), custom_call_target="tpu_custom_call" | custom-call | tf_op jit(solution)/shard_map/block/pallas_call | solution.py:444
  68.8 0.7 %copy.9 = bf16[2,16,8,288]{3,2,1,0:T(8,128)(2,1)} copy(bf16[2,16,8,288]{3,2,0,1:T(8,128)(2,1)S(1)} %bitcast.11) | data formatting | bytes 294912 | tf_op jit(solution)/shard_map/transpose | solution.py:490

commit v5 on v4

--- a/solution.py
+++ b/solution.py
@@ -15,9 +15,14 @@
 MESH = pl.DeviceIdType.MESH
 F32 = jnp.float32
 BF16 = jnp.bfloat16
-CUT = 1
+CUT = 2
 RUN = 32 // CUT
-ORDER = [(k, n, 0) for k in range(6) for n in range(2)]
+ORDER = [
+    (0, 0, 0), (0, 1, 0), (1, 0, 0), (1, 1, 0),
+    (2, 0, 0), (2, 0, 1), (2, 1, 0), (2, 1, 1),
+    (3, 0, 0), (3, 0, 1), (3, 1, 0), (3, 1, 1),
+    (4, 0, 0), (4, 1, 0), (5, 0, 0), (5, 1, 0),
+]
 
 
 def dot(a, b):
@@ -97,7 +102,7 @@
     mod, w_s, w_so, w_t, w_to, w_up, w_dn, w_dp, c_s, c_t,
     lv, lp, g, lfull, qb, kvf, hp, halo, ps, r4, lsel, pk, a2, blk, pt, r7, blk2, pmp, r8, fin,
     spread_sel, unpack_sel, turn,
-    wsem, s1, d1, sh, dh, s4, d4, s5, d5, s6, d6, s7, d7, s7b, d7b, s8, d8, s9, d9, zsem, ysem, xsem, csem,
+    wsem, s1, d1, sh, dh, s4, d4, s5, d5, s6, d6, s7, d7, s7b, d7b, s8, d8, s9, d9, asem, zsem, ysem, xsem, csem,
 ):
     tm = lax.axis_index("tm")
     he = lax.axis_index("height")
@@ -170,9 +175,10 @@
         for i in range(2):
             tell(first_peer(i, k))
     for k in range(1, 4):
-        tell(xdev(k))
-        tell(dev(zlo, c, zhi, (y + k) % 4, x))
-    tell(dev(zlo, 1 - c, zhi, y, x))
+        pl.when(x + k < 4)(lambda k=k: tell(dev(zlo, c, zhi, y, x + k)))
+        pl.when(y + k < 4)(lambda k=k: tell(dev(zlo, c, zhi, y + k, x)))
+    core_dev = dev(zlo, 1 - c, zhi, y, x)
+    pl.when(c == 0)(lambda: tell(core_dev))
 
     for k in range(1, 4):
         pl.when(zlo + k < 4)(lambda k=k: tell(z_dev(zlo + k)))
@@ -184,13 +190,15 @@
         for i in range(2):
             tell(first_peer(i, 0))
 
+    pl.when(at_home)(lambda: tell(first_peer(1 - y % 2, 0)))
+
     for k in (6, 0, 5, 2, 1, 3, 4):
         loads[k].start()
 
     loads[7].wait()
     for i in range(2):
         lp[i] = pack_part(lv[i].astype(F32)).astype(BF16)
-    pl.semaphore_wait(bar, 13 + zlo + jnp.where(cross & (zhi == 1), 1, 0) + jnp.where(away, 2, 0))
+    pl.semaphore_wait(bar, 6 + x + y + c + zlo + jnp.where(cross & (zhi == 1), 1, 0) + jnp.where(away, 2, 1))
 
     slot = y % 2
 
@@ -213,7 +221,9 @@
         pl.semaphore_signal(semaphore, inc=1, device_id=device, device_id_type=MESH)
 
     for k in range(1, 4):
-        pl.when(zlo >= k)(lambda k=k: answer(zsem, z_dev(zlo - k)))
+        pl.when(x >= k)(lambda k=k: answer(asem, dev(zlo, c, zhi, y, x - k)))
+        pl.when(y >= k)(lambda k=k: answer(asem, dev(zlo, c, zhi, y - k, x)))
+    pl.when(c == 1)(lambda: answer(asem, core_dev))
     pl.when(cross & (zhi == 1))(lambda: answer(xsem, cross_dev))
 
     q_masks = lane_masks(PART, 0)
@@ -276,6 +286,10 @@
 
     first, second = row_of[1], row_of[0]
     normed_first = prepare(first)
+    waits = 7 - x - y - c
+    pl.when(waits > 0)(lambda: pl.semaphore_wait(asem, waits))
+    for k in range(1, 4):
+        pl.when(zlo >= k)(lambda k=k: answer(zsem, z_dev(zlo - k)))
     pl.when(cross & (zhi == 0))(lambda: pl.semaphore_wait(xsem, 1))
     outer = remote(hp.at[row_b], halo.at[1], sh.at[1], dh.at[1], cross_dev)
     inner = remote(hp.at[row_a], halo.at[0], sh.at[0], dh.at[0], dev(zlo, 1 - c, zhi, y, x))
@@ -301,9 +315,6 @@
                 ps.at[n, pl.ds(((x + k) % 4) * 32, 32)], r4.at[n, x], s4.at[n * 4 + k], d4.at[n * 4 + x], xdev(k)
             ))
 
-    pl.when(zlo < 3)(lambda: pl.semaphore_wait(zsem, 3 - zlo))
-    for k in range(1, 4):
-        pl.when(zlo + k < 4)(lambda k=k: answer(ysem, z_dev(zlo + k)))
     pl.when(cross)(lambda: arrived(halo.at[0], dh.at[0]))
     spatial(0, jnp.where(cross, 0.0, -1e30))
     for n in range(2):
@@ -312,6 +323,9 @@
     pl.when(cross)(lambda: arrived(halo.at[1], dh.at[1]))
     pl.when(jnp.logical_not(cross))(lambda: arrived(halo.at[0], dh.at[0]))
     spatial(1, 0.0)
+    pl.when(zlo < 3)(lambda: pl.semaphore_wait(zsem, 3 - zlo))
+    for k in range(1, 4):
+        pl.when(zlo + k < 4)(lambda k=k: answer(ysem, z_dev(zlo + k)))
     pl.when(zlo > 0)(lambda: pl.semaphore_wait(ysem, zlo))
 
     def gather(buf, i, ssem, rsem):
@@ -475,7 +489,7 @@
             sem((8,)), sem((8,)), sem((2,)), sem((2,)), sem((8,)), sem((8,)), sem((32,)), sem((32,)),
             sem((8 * CUT,)), sem((8 * CUT,)), sem((8 * CUT,)), sem((8 * CUT,)), sem((8 * CUT,)), sem((8 * CUT,)),
             sem((8,)), sem((8,)), sem((16,)), sem((16,)),
-            pltpu.SemaphoreType.REGULAR, pltpu.SemaphoreType.REGULAR,
+            pltpu.SemaphoreType.REGULAR, pltpu.SemaphoreType.REGULAR, pltpu.SemaphoreType.REGULAR,
             pltpu.SemaphoreType.REGULAR, pltpu.SemaphoreType.REGULAR,
         ],
         compiler_params=pltpu.CompilerParams(

time: 69.6 us -> 68.3 us (0.981)
  the two profiles are of different devices: /device:TPU:9 before, /device:TPU:1 now
where the time goes in v5:
time: 68.3 us; the launch traced here: 67.5 us
  Pallas kernels  66.8 us (98%)
  local copies, waits for them, and re-layouts  0.7 us (1%)
    pallas_call x1, Pallas kernels, body(): pl.pallas_call(kernel, out_shape=pltpu.VMEM((16, 16, PART), BF16), in_spe...  66.8 us

profile of v5, /device:TPU:1, one launch (start us, length us, event | category | flops | bytes accessed | tf_op | source)
XLA Modules:
  0.0 67.5 jit_solution(12802918016931250678)
XLA Ops:
  0.0 66.8 %block.1 = bf16[16,16,288]{2,1,0:T(8,128)(2,1)S(1)} custom-call(bf16[2,128,288]{2,1,0:T(8,128)(2,1)} %bitcast.14, f32[9,1152]{1,0:T(8,128)} %mod_h.1, bf16[864,1152]{1,0:T(8,128)(2,1)} %bitcast.12, bf16[288,1152]{1,0:T(8,128)(2,1)} %wo_h.1, bf16[864,1152]{1,0:T(8,128)(2,1)} %bitcast.13, bf16[288,1152]{1,0:T(8,128)(2,1)} %to_h.1, bf16[1152,1152]{1,0:T(8,128)(2,1)} %up_h.1, ...), custom_call_target="tpu_custom_call" | custom-call | tf_op jit(solution)/shard_map/block/pallas_call | solution.py:458
  66.8 0.7 %copy.9 = bf16[2,16,8,288]{3,2,1,0:T(8,128)(2,1)} copy(bf16[2,16,8,288]{3,2,0,1:T(8,128)(2,1)S(1)} %bitcast.11) | data formatting | bytes 294912 | tf_op jit(solution)/shard_map/transpose | solution.py:504

commit v6 on v5

--- a/solution.py
+++ b/solution.py
@@ -402,8 +402,9 @@
                 [out[:, 256 * xd : 256 * xd + 128], out[:, 256 * xd + 128 : 256 * xd + 256],
                  jnp.concatenate(rest, axis=1)], axis=0,
             ).astype(BF16)
-        for k in (2, 1, 3):
-            send(remote(pmp.at[n, (x + k) % 4], r8.at[n, x], s8.at[n * 4 + k], d8.at[n * 4 + x], xdev(k)))
+            send_if(x != xd, remote(
+                pmp.at[n, xd], r8.at[n, x], s8.at[n * 4 + xd], d8.at[n * 4 + x], dev(zlo, c, zhi, y, xd)
+            ))
 
     def stage_return(n, u):
         lanes = pl.ds(pl.multiple_of(x * 256, 128), COVER)

time: 68.3 us -> 68.3 us (level)
  no operation moved by 1% of the time
where the time goes in v6:
time: 68.3 us; the launch traced here: 67.5 us
  Pallas kernels  66.8 us (98%)
  local copies, waits for them, and re-layouts  0.7 us (1%)
    pallas_call x1, Pallas kernels, body(): pl.pallas_call(kernel, out_shape=pltpu.VMEM((16, 16, PART), BF16), in_spe...  66.8 us

profile of v6, /device:TPU:1, one launch (start us, length us, event | category | flops | bytes accessed | tf_op | source)
XLA Modules:
  0.0 67.5 jit_solution(13442122918974701532)
XLA Ops:
  0.0 66.8 %block.1 = bf16[16,16,288]{2,1,0:T(8,128)(2,1)S(1)} custom-call(bf16[2,128,288]{2,1,0:T(8,128)(2,1)} %bitcast.14, f32[9,1152]{1,0:T(8,128)} %mod_h.1, bf16[864,1152]{1,0:T(8,128)(2,1)} %bitcast.12, bf16[288,1152]{1,0:T(8,128)(2,1)} %wo_h.1, bf16[864,1152]{1,0:T(8,128)(2,1)} %bitcast.13, bf16[288,1152]{1,0:T(8,128)(2,1)} %to_h.1, bf16[1152,1152]{1,0:T(8,128)(2,1)} %up_h.1, ...), custom_call_target="tpu_custom_call" | custom-call | tf_op jit(solution)/shard_map/block/pallas_call | solution.py:459
  66.8 0.7 %copy.9 = bf16[2,16,8,288]{3,2,1,0:T(8,128)(2,1)} copy(bf16[2,16,8,288]{3,2,0,1:T(8,128)(2,1)S(1)} %bitcast.11) | data formatting | bytes 294912 | tf_op jit(solution)/shard_map/transpose | solution.py:505
